TPU v7x, 32 devices: a whole 2x2x4 slice. The times are simulated.
32 devices in a mesh: gz: 16 (over z, y, core), gy: 2 (over x).
Axes of the slice: x: 2, y: 2, z: 4, core: 2. Of those that a mesh axis runs over, the one named last changes fastest.
Arguments:
- density: float32 [160, 32, 2048], P('gz', 'gy'), may hold values from -6 to 6
- dilations: int32 [3], replicated, may hold values from 1 to 4, as said below
- owner_rank: int32 [8192, 1], P(('gz', 'gy')), may hold values from 0 to 1; in each aligned block of 256 rows (0 to 255, 256 to 511, ...) at most 128 rows name the same one
- owner_slot: int32 [8192], P(('gz', 'gy')), may hold values from 0 to 255
- base_cell: int32 [8192], P(('gz', 'gy')), may hold values from 0 to 276479
- corner_weights: float32 [8, 8192], P(None, ('gz', 'gy')), may hold values from 0.05 to 1
Outputs:
- response: float32 [160, 32, 2048], P('gz', 'gy')
- catalogue: float32 [3, 8192], P(None, ('gz', 'gy'))
Inputs may be any that keep to these rules, and one draw needn't show every extreme that they name: `dilations`: one level has dilation 4 and another has dilation 1. `owner_rank`: the entries listed on one device name one owner at most 128 times; some owner is named exactly 128 times by some device.
All inputs are finite; a program needn't handle non-finite values.
Results may differ from a plain program's by a relative error of at most 0.00014.
Values sent between devices are 32-bit elements; how exact they have to be, the bound alone decides.
A program may use at most 192 MiB of HBM per device.

v0:
```python
import jax
import jax.numpy as jnp
from jax import lax
from jax.sharding import PartitionSpec as P

SCALES = 3
HALO = 9
HOWN = 256


tap_weights = (0.0625, 0.25, 0.375, 0.25, 0.0625)
hessian_scale = 4.0


def with_halo(block, sides, width):
    for axis, dim in sides:
        count = lax.axis_size(axis)
        forward = [(i, i + 1) for i in range(count - 1)]
        forward.append((count - 1, 0))
        backward = [(target, source) for source, target in forward]
        low = lax.ppermute(
            lax.slice_in_dim(block, block.shape[dim] - width, None, axis=dim), axis, forward
        )
        high = lax.ppermute(lax.slice_in_dim(block, 0, width, axis=dim), axis, backward)
        block = jnp.concatenate([low, block, high], axis=dim)
    return block


def smooth_padded(field_data, dilation, along_dim, extent):
    running = None
    for offset in range(5):
        start_at = HALO - 1 + (offset - 2) * dilation
        summand = tap_weights[offset] * lax.dynamic_slice_in_dim(
            field_data, start_at, extent + 2, along_dim
        )
        running = summand if running is None else running + summand
    return running


def smooth_periodic(field_data, dilation):
    running = None
    for offset in range(5):
        summand = tap_weights[offset] * jnp.roll(field_data, -(offset - 2) * dilation, axis=2)
        running = summand if running is None else running + summand
    return running


def invariants(curve_zz, curve_yy, curve_xx, curve_zy, curve_zx, curve_yx):
    trace_sum = curve_xx + curve_yy + curve_zz
    minor_sum = (
        curve_xx * curve_yy
        + curve_xx * curve_zz
        + curve_yy * curve_zz
        - curve_zy * curve_zy
        - curve_zx * curve_zx
        - curve_yx * curve_yx
    )
    return (trace_sum * trace_sum / 3.0 - minor_sum) * jax.nn.sigmoid(-trace_sum)


def signature(smoothed):
    centre = smoothed[1:-1, 1:-1]
    above_z = smoothed[2:, 1:-1]
    below_z = smoothed[:-2, 1:-1]
    above_y = smoothed[1:-1, 2:]
    below_y = smoothed[1:-1, :-2]
    curve_zz = hessian_scale * (above_z - 2.0 * centre + below_z)
    curve_yy = hessian_scale * (above_y - 2.0 * centre + below_y)
    curve_xx = hessian_scale * (jnp.roll(centre, -1, 2) - 2.0 * centre + jnp.roll(centre, 1, 2))
    curve_zy = (
        hessian_scale
        * 0.25
        * (smoothed[2:, 2:] - smoothed[2:, :-2] - smoothed[:-2, 2:] + smoothed[:-2, :-2])
    )
    curve_zx = (
        hessian_scale
        * 0.25
        * (
            jnp.roll(above_z, -1, 2)
            - jnp.roll(above_z, 1, 2)
            - jnp.roll(below_z, -1, 2)
            + jnp.roll(below_z, 1, 2)
        )
    )
    curve_yx = (
        hessian_scale
        * 0.25
        * (
            jnp.roll(above_y, -1, 2)
            - jnp.roll(above_y, 1, 2)
            - jnp.roll(below_y, -1, 2)
            + jnp.roll(below_y, 1, 2)
        )
    )
    return invariants(curve_zz, curve_yy, curve_xx, curve_zy, curve_zx, curve_yx)


def per_device(density, dilations, owner_rank, owner_slot, base_cell, corner_weights):
    slab_depth = density.shape[0]
    band_rows = density.shape[1]
    row_length = density.shape[2]
    banded = with_halo(density, (("gy", 1),), HALO)
    response = None
    levels = []
    for level_index in range(SCALES):
        dilation = dilations[level_index]
        along_y = with_halo(smooth_padded(banded, dilation, 1, band_rows), (("gz", 0),), HALO)
        along_z = smooth_padded(along_y, dilation, 0, slab_depth)
        smoothed = smooth_periodic(along_z, dilation)
        feature = signature(smoothed)
        response = feature if response is None else jnp.maximum(response, feature)
        levels.append(feature.reshape(-1))
    feature_table = jnp.stack(levels)
    plane = (band_rows - 1) * row_length
    z_index = base_cell // plane
    remainder = base_cell % plane
    y_index = remainder // row_length
    x_index = remainder % row_length
    partial_value = None
    corner = 0
    for step_z in (0, 1):
        for step_y in (0, 1):
            for step_x in (0, 1):
                cell_index = (
                    (z_index + step_z) * (band_rows * row_length)
                    + (y_index + step_y) * row_length
                    + (x_index + step_x) % row_length
                )
                summand = corner_weights[corner] * feature_table[:, cell_index]
                partial_value = summand if partial_value is None else partial_value + summand
                corner += 1
    owner_group = owner_rank[:, 0]
    groups = lax.axis_size("gy")
    column = owner_group * HOWN + owner_slot
    onehot = (column[:, None] == jnp.arange(groups * HOWN, dtype=jnp.int32)[None, :]).astype(
        jnp.float32
    )
    spread = jnp.dot(
        partial_value, onehot, precision=lax.Precision.HIGHEST, preferred_element_type=jnp.float32
    )
    catalogue = lax.psum_scatter(spread, "gy", scatter_dimension=1, tiled=True)
    return (response, catalogue)


def solution(mesh):
    placed = (
        P("gz", "gy", None),
        P(),
        P(("gz", "gy"), None),
        P(("gz", "gy")),
        P(("gz", "gy")),
        P(None, ("gz", "gy")),
    )
    return jax.shard_map(
        per_device,
        mesh=mesh,
        in_specs=placed,
        out_specs=(P("gz", "gy", None), P(None, ("gz", "gy"))),
        check_vma=False,
    )
```

profile of v0, /device:TPU:0, one launch (start us, length us, event | category | flops | bytes accessed | tf_op | source)
XLA Modules:
  0.0 334.7 jit_solution(14118747909237959458)
XLA Ops:
  7.2 2.0 fusion.132
  9.6 3.0 collective-permute-start
  23.6 1.3 compare_select_fusion.7
  25.6 1.3 compare_select_fusion.5
  28.1 1.2 broadcast_multiply_fusion
  30.0 9.5 %collective-permute-done = f32[10,9,2048]{2,0,1:T(8,128)S(1)} collective-permute-done((f32[10,9,2048]{2,0,1:T(8,128)S(1)}, f32[10,9,2048]{2,0,1:T(8,128)S(1)}, u32[]{:S(2)}, u32[]{:S(2)}) %collective-permute-start) | collective-permute-done | bytes 737312 | tf_op jit(solution)/shard_map/ppermute | solution.py:21
  39.9 24.1 %collective-permute-done.1 = f32[10,9,2048]{2,0,1:T(8,128)} collective-permute-done((f32[10,9,2048]{2,0,1:T(8,128)S(1)}, f32[10,9,2048]{2,0,1:T(8,128)}, u32[]{:S(2)}, u32[]{:S(2)}) %collective-permute-start.1) | collective-permute-done | bytes 737312 | tf_op jit(solution)/shard_map/ppermute | solution.py:24
  64.0 1.7 copy.11
  66.2 5.9 %multiply_add_fusion = (f32[10,18,2048]{2,1,0:T(8,128)S(1)}, f32[10,18,2048]{2,1,0:T(8,128)}, f32[10,18,2048]{2,1,0:T(8,128)S(1)}) fusion(f32[10,34,2048]{2,1,0:T(8,128)S(1)} %pad_maximum_fusion.4, s32[]{:T(128)S(6)} %select_n.166, s32[]{:T(128)S(6)} %select_n.165, s32[]{:T(128)S(6)} %select_n.164, s32[]{:T(128)S(6)} %select_n.163, s32[]{:T(128)S(6)} %select_n.158, ...), kind=kLoop, calls=%fused_computation.86 | loop fusion | flops 9216000 | bytes 23593008 | tf_op jit(solution)/shard_map/add | solution.py:36
  72.1 2.5 fusion.130
  74.7 4.4 %collective-permute-start.3 = (f32[9,18,2048]{2,1,0:T(8,128)}, f32[9,18,2048]{2,1,0:T(8,128)}, u32[]{:S(2)}, u32[]{:S(2)}) collective-permute-start(f32[9,18,2048]{2,1,0:T(8,128)} %get-tuple-element.81), channel_id=1, source_target_pairs={{2,0},{4,2},{6,4},{8,6},{10,8},{12,10},{14,12},{16,14},{18,16},{20... | collective-permute-start | bytes 3981320 | tf_op jit(solution)/shard_map/ppermute | solution.py:24
  87.3 4.2 %fusion.131 = (f32[9,18,2048]{2,1,0:T(8,128)}, f32[9,18,2048]{2,1,0:T(8,128)}) fusion(f32[10,18,2048]{2,1,0:T(8,128)} %get-tuple-element.16), kind=kLoop, calls=%fused_computation.250 | loop fusion | bytes 5308416 | tf_op jit(solution)/shard_map/slice | solution.py:22
  91.4 4.4 %collective-permute-start.5 = (f32[9,18,2048]{2,1,0:T(8,128)}, f32[9,18,2048]{2,1,0:T(8,128)}, u32[]{:S(2)}, u32[]{:S(2)}) collective-permute-start(f32[9,18,2048]{2,1,0:T(8,128)} %get-tuple-element.83), channel_id=1, source_target_pairs={{2,0},{4,2},{6,4},{8,6},{10,8},{12,10},{14,12},{16,14},{18,16},{20... | collective-permute-start | bytes 3981320 | tf_op jit(solution)/shard_map/ppermute | solution.py:24
  95.9 2.2 fusion.129
  98.1 1.7 collective-permute-done.2
  99.7 2.9 collective-permute-start.7
  102.7 2.7 pad_maximum_fusion
  105.4 1.3 fusion.44
  106.8 5.1 %fusion.26 = f32[12,18,2048]{2,1,0:T(8,128)S(1)} fusion(s32[]{:T(128)S(6)} %select_n.214, f32[12,18,2048]{2,1,0:T(8,128)S(1)} %fusion.44, s32[]{:T(128)S(6)} %select_n.208, s32[]{:T(128)S(6)} %select_n.210, s32[]{:T(128)S(6)} %select_n.212), kind=kLoop, calls=%fused_computation.63 | loop fusion | flops 5750784 | bytes 3538960 | tf_op jit(solution)/shard_map/add | solution.py:44
  112.1 6.6 %collective-permute-done.4 = f32[9,18,2048]{2,1,0:T(8,128)} collective-permute-done((f32[9,18,2048]{2,1,0:T(8,128)}, f32[9,18,2048]{2,1,0:T(8,128)}, u32[]{:S(2)}, u32[]{:S(2)}) %collective-permute-start.4) | collective-permute-done | bytes 1327136 | tf_op jit(solution)/shard_map/ppermute | solution.py:21
  118.7 2.5 pad_maximum_fusion.1
  121.3 2.8 fusion.41
  124.0 6.6 %fusion.125 = (f32[10,16,2047]{2,1,0:T(8,128)}, f32[10,16,2047]{2,1,0:T(8,128)}, f32[10,16,2047]{2,1,0:T(8,128)}, f32[10,16,2047]{2,1,0:T(8,128)}, f32[10,16,204...) fusion(f32[12,18,2048]{2,1,0:T(8,128)S(1)} %fusion.26), kind=kLoop, calls=%fused_computation.244 | loop fusion | bytes 26201600 | tf_op jit(solution)/shard_map/jit(_roll_static)/slice | solution.py:69
  130.6 7.1 %collective-permute-done.6 = f32[9,18,2048]{2,1,0:T(8,128)} collective-permute-done((f32[9,18,2048]{2,1,0:T(8,128)}, f32[9,18,2048]{2,1,0:T(8,128)}, u32[]{:S(2)}, u32[]{:S(2)}) %collective-permute-start.6) | collective-permute-done | bytes 1327136 | tf_op jit(solution)/shard_map/ppermute | solution.py:21
  137.7 19.2 %collective-permute-done.7 = f32[9,18,2048]{2,1,0:T(8,128)} collective-permute-done((f32[9,18,2048]{2,1,0:T(8,128)}, f32[9,18,2048]{2,1,0:T(8,128)}, u32[]{:S(2)}, u32[]{:S(2)}) %collective-permute-start.7) | collective-permute-done | bytes 1327136 | tf_op jit(solution)/shard_map/ppermute | solution.py:24
  156.9 3.2 pad_maximum_fusion.2
  160.2 1.7 fusion.38
  161.9 12.6 %fusion.2 = (f32[12,18,2048]{2,1,0:T(8,128)}, f32[12,18,2048]{2,1,0:T(8,128)}) fusion(s32[]{:T(128)S(6)} %select_n.230, f32[12,18,2048]{2,1,0:T(8,128)S(1)} %fusion.38, s32[]{:T(128)S(6)} %select_n.224, s32[]{:T(128)S(6)} %select_n.226, s32[]{:T(128)S(6)} %select_n.228, s32[]{:T(128)S(6)} %select_n.222, s32[]{:T(128)S(6)} %select_n.220, ...), kind=kLoop, calls=%fused_computation.39 | loop fusion | flops 11501568 | bytes 7077920 | tf_op jit(solution)/shard_map/add | solution.py:44
  174.5 14.7 %fusion.123 = (f32[10,16,2047]{2,1,0:T(8,128)}, f32[10,16,2047]{2,1,0:T(8,128)}, f32[10,16,2047]{2,1,0:T(8,128)}, f32[10,16,2047]{2,1,0:T(8,128)}, f32[10,16,204...) fusion(f32[12,18,2048]{2,1,0:T(8,128)} %get-tuple-element.106), kind=kLoop, calls=%fused_computation.242 | loop fusion | bytes 26201600 | tf_op jit(solution)/shard_map/jit(_roll_static)/slice | solution.py:69
  189.2 2.5 fusion.124
  191.7 13.7 %fusion.127 = (f32[10,16,2047]{2,1,0:T(8,128)}, f32[10,16,2047]{2,1,0:T(8,128)}, f32[10,16,2047]{2,1,0:T(8,128)}, f32[10,16,2047]{2,1,0:T(8,128)}, f32[10,16,204...) fusion(f32[12,18,2048]{2,1,0:T(8,128)} %get-tuple-element.107), kind=kLoop, calls=%fused_computation.246 | loop fusion | bytes 26201600 | tf_op jit(solution)/shard_map/jit(_roll_static)/slice | solution.py:69
  205.5 1.8 fusion.128
  207.3 31.9 %maximum_maximum_fusion = (f32[10,16,2048]{2,1,0:T(8,128)}, f32[10,16,2048]{2,1,0:T(8,128)}, f32[10,16,2048]{2,1,0:T(8,128)}, f32[10,16,2048]{2,1,0:T(8,128)}) fusion(f32[10,16,2047]{2,1,0:T(8,128)} %get-tuple-element.63, f32[10,16,1]{2,1,0:T(8,128)S(1)} %get-tuple-element.73, f32[10,16,1]{2,1,0:T(8,128)S(1)} %get-tuple-element.74, ...), kind=kLoop, calls=%fused_computation.173 | loop fusion | flops 46858240 | bytes 79953920 | tf_op jit(solution)/shard_map/max | solution.py:111
  239.2 2.9 stack_reshape.10
  242.1 2.9 stack_reshape.11
  245.0 4.0 %stack_reshape.9 = f32[1,327680]{1,0:T(1,128)} reshape(f32[10,16,2048]{2,1,0:T(8,128)} %get-tuple-element.13) | data formatting | bytes 2621440 | tf_op jit(solution)/shard_map/stack;reshape | solution.py:113
  248.9 6.0 %pad_maximum_fusion.3 = f32[3,327680]{1,0:T(4,128)} fusion(f32[1,327680]{1,0:T(1,128)S(1)} %stack_reshape.11, f32[1,327680]{1,0:T(1,128)S(1)} %stack_reshape.10, f32[1,327680]{1,0:T(1,128)} %stack_reshape.9), kind=kLoop, calls=%fused_computation.35 | loop fusion | flops 1966080 | bytes 7864320 | tf_op jit(solution)/shard_map/stack | solution.py:113
  254.9 2.7 gather_fusion.2
  257.6 2.6 gather_fusion.3
  260.2 2.7 gather_fusion.4
  263.1 2.7 gather_fusion.5
  265.8 2.6 gather_fusion.6
  268.4 2.8 gather_fusion.1
  271.2 2.6 gather_fusion.7
  273.8 2.6 gather_fusion
  276.5 1.4 convolution_bitcast_fusion
  277.9 48.2 %reduce-scatter.4.cloned.1.call-done = f32[256,3]{1,0:T(8,128)} async-done(((f32[512,3]{1,0:T(8,128)}), f32[256,3]{1,0:T(8,128)}) %reduce-scatter.4.cloned.1.call-update) | async-done | bytes 3088
  326.1 1.6 copy.13
  (76 shorter events, 5.4 us)
Async XLA Ops:
  7.2 318.9 %reduce-scatter.4.cloned.1.call-start = ((), (), s32[]{:S(2)}) async-start(), calls=%async_computation.1 | async-start | bytes 393216
  9.6 3.6 %copy-start.13 = (s32[3]{0:T(128)S(1)}, s32[3]{0:T(128)}, u32[]{:S(2)}) copy-start(s32[3]{0:T(128)} %param.11) | copy-start | bytes 40
  9.6 29.8 %collective-permute-start = (f32[10,9,2048]{2,0,1:T(8,128)S(1)}, f32[10,9,2048]{2,0,1:T(8,128)S(1)}, u32[]{:S(2)}, u32[]{:S(2)}) collective-permute-start(f32[10,9,2048]{2,0,1:T(8,128)S(1)} %copy.14), channel_id=1, source_target_pairs={{0,1},{1,0},{2,3},{3,2},{4,5},{5,4},{6,7},{7,6},{8,9},{9,8},{10,11... | collective-permute-start | bytes 2211848 | tf_op jit(solution)/shard_map/ppermute | solution.py:21
  12.7 16.7 %copy-start.12 = (f32[8,256]{1,0:T(8,128)S(1)}, f32[8,256]{1,0:T(8,128)}, u32[]{:S(2)}) copy-start(f32[8,256]{1,0:T(8,128)} %param.15) | copy-start | bytes 24580
  13.1 50.9 %collective-permute-start.1 = (f32[10,9,2048]{2,0,1:T(8,128)S(1)}, f32[10,9,2048]{2,0,1:T(8,128)}, u32[]{:S(2)}, u32[]{:S(2)}) collective-permute-start(f32[10,9,2048]{2,0,1:T(8,128)S(1)} %copy.15), channel_id=1, source_target_pairs={{1,0},{0,1},{3,2},{2,3},{5,4},{4,5},{7,6},{6,7},{9,8},{8,9},{11,10... | collective-permute-start | bytes 2211848 | tf_op jit(solution)/shard_map/ppermute | solution.py:24
  39.9 25.8 %copy-start.4 = (f32[10,16,2048]{2,1,0:T(8,128)S(1)}, f32[10,16,2048]{2,1,0:T(8,128)}, u32[]{:S(2)}) copy-start(f32[10,16,2048]{2,1,0:T(8,128)} %param.10) | copy-start | bytes 3932164
  72.1 2.6 copy-start.2
  72.1 23.8 %copy-start = (f32[10,18,2048]{2,1,0:T(8,128)}, f32[10,18,2048]{2,1,0:T(8,128)S(1)}, u32[]{:S(2)}) copy-start(f32[10,18,2048]{2,1,0:T(8,128)S(1)} %get-tuple-element.15) | copy-start | bytes 4423684
  72.1 7.0 %copy-start.25 = (s32[256]{0:T(256)S(1)}, s32[256]{0:T(256)}, u32[]{:S(2)}) copy-start(s32[256]{0:T(256)} %get-tuple-element.4) | copy-start | bytes 3076
  72.1 15.1 %copy-start.24 = (s32[256,1]{0,1:T(1,128)S(1)}, s32[256,1]{0,1:T(1,128)}, u32[]{:S(2)}) copy-start(s32[256,1]{0,1:T(1,128)} %broadcast_multiply_fusion) | copy-start | bytes 3076
  72.1 15.1 %copy-start.26 = (s32[256]{0:T(256)S(1)}, s32[256]{0:T(256)}, u32[]{:S(2)}) copy-start(s32[256]{0:T(256)} %param.13) | copy-start | bytes 3076
  72.1 15.1 %copy-start.22 = (s32[256]{0:T(256)S(1)}, s32[256]{0:T(256)}, u32[]{:S(2)}) copy-start(s32[256]{0:T(256)} %get-tuple-element.96) | copy-start | bytes 3076
  72.1 15.1 %copy-start.23 = (s32[256]{0:T(256)S(1)}, s32[256]{0:T(256)}, u32[]{:S(2)}) copy-start(s32[256]{0:T(256)} %get-tuple-element.100) | copy-start | bytes 3076
  74.7 25.1 %collective-permute-start.2 = (f32[9,18,2048]{2,1,0:T(8,128)}, f32[9,18,2048]{2,1,0:T(8,128)}, u32[]{:S(2)}, u32[]{:S(2)}) collective-permute-start(f32[9,18,2048]{2,1,0:T(8,128)} %get-tuple-element.80), channel_id=1, source_target_pairs={{0,2},{2,4},{4,6},{6,8},{8,10},{10,12},{12,14},{14,16},{16,18},{18... | collective-permute-start | bytes 3981320 | tf_op jit(solution)/shard_map/ppermute | solution.py:21
  74.7 28.0 %collective-permute-start.3 = (f32[9,18,2048]{2,1,0:T(8,128)}, f32[9,18,2048]{2,1,0:T(8,128)}, u32[]{:S(2)}, u32[]{:S(2)}) collective-permute-start(f32[9,18,2048]{2,1,0:T(8,128)} %get-tuple-element.81), channel_id=1, source_target_pairs={{2,0},{4,2},{6,4},{8,6},{10,8},{12,10},{14,12},{16,14},{18,16},{20... | collective-permute-start | bytes 3981320 | tf_op jit(solution)/shard_map/ppermute | solution.py:24
  91.4 27.3 %collective-permute-start.4 = (f32[9,18,2048]{2,1,0:T(8,128)}, f32[9,18,2048]{2,1,0:T(8,128)}, u32[]{:S(2)}, u32[]{:S(2)}) collective-permute-start(f32[9,18,2048]{2,1,0:T(8,128)} %get-tuple-element.82), channel_id=1, source_target_pairs={{0,2},{2,4},{4,6},{6,8},{8,10},{10,12},{12,14},{14,16},{16,18},{18... | collective-permute-start | bytes 3981320 | tf_op jit(solution)/shard_map/ppermute | solution.py:21
  91.4 27.3 %collective-permute-start.5 = (f32[9,18,2048]{2,1,0:T(8,128)}, f32[9,18,2048]{2,1,0:T(8,128)}, u32[]{:S(2)}, u32[]{:S(2)}) collective-permute-start(f32[9,18,2048]{2,1,0:T(8,128)} %get-tuple-element.83), channel_id=1, source_target_pairs={{2,0},{4,2},{6,4},{8,6},{10,8},{12,10},{14,12},{16,14},{18,16},{20... | collective-permute-start | bytes 3981320 | tf_op jit(solution)/shard_map/ppermute | solution.py:24
  95.9 6.8 %copy-start.3 = (f32[10,18,2048]{2,1,0:T(8,128)S(1)}, f32[10,18,2048]{2,1,0:T(8,128)}, u32[]{:S(2)}) copy-start(f32[10,18,2048]{2,1,0:T(8,128)} %copy-done.2) | copy-start | bytes 4423684
  98.1 39.6 %collective-permute-start.6 = (f32[9,18,2048]{2,1,0:T(8,128)}, f32[9,18,2048]{2,1,0:T(8,128)}, u32[]{:S(2)}, u32[]{:S(2)}) collective-permute-start(f32[9,18,2048]{2,1,0:T(8,128)} %get-tuple-element.78), channel_id=1, source_target_pairs={{0,2},{2,4},{4,6},{6,8},{8,10},{10,12},{12,14},{14,16},{16,18},{18... | collective-permute-start | bytes 3981320 | tf_op jit(solution)/shard_map/ppermute | solution.py:21
  99.7 57.2 %collective-permute-start.7 = (f32[9,18,2048]{2,1,0:T(8,128)}, f32[9,18,2048]{2,1,0:T(8,128)}, u32[]{:S(2)}, u32[]{:S(2)}) collective-permute-start(f32[9,18,2048]{2,1,0:T(8,128)} %get-tuple-element.79), channel_id=1, source_target_pairs={{2,0},{4,2},{6,4},{8,6},{10,8},{12,10},{14,12},{16,14},{18,16},{20... | collective-permute-start | bytes 3981320 | tf_op jit(solution)/shard_map/ppermute | solution.py:24
  106.7 12.0 %copy-start.1 = (f32[10,18,2048]{2,1,0:T(8,128)S(1)}, f32[10,18,2048]{2,1,0:T(8,128)}, u32[]{:S(2)}) copy-start(f32[10,18,2048]{2,1,0:T(8,128)} %get-tuple-element.16) | copy-start | bytes 4423684
  160.2 1.8 copy-start.5
  205.4 1.8 copy-start.6
  205.4 1.9 copy-start.7
  205.4 1.9 copy-start.8
  205.4 1.9 copy-start.9
  205.5 1.9 copy-start.10
  205.5 1.9 copy-start.11
  263.0 13.4 %copy-start.14 = (f32[1,256]{1,0:T(1,128)S(1)}, f32[1,256]{1,0:T(1,128)}, u32[]{:S(2)}) copy-start(f32[1,256]{1,0:T(1,128)} %get-tuple-element.86) | copy-start | bytes 3076
  263.0 13.4 %copy-start.15 = (f32[1,256]{1,0:T(1,128)S(1)}, f32[1,256]{1,0:T(1,128)}, u32[]{:S(2)}) copy-start(f32[1,256]{1,0:T(1,128)} %get-tuple-element.87) | copy-start | bytes 3076
  263.0 13.4 %copy-start.16 = (f32[1,256]{1,0:T(1,128)S(1)}, f32[1,256]{1,0:T(1,128)}, u32[]{:S(2)}) copy-start(f32[1,256]{1,0:T(1,128)} %get-tuple-element.88) | copy-start | bytes 3076
  263.0 13.4 %copy-start.17 = (f32[1,256]{1,0:T(1,128)S(1)}, f32[1,256]{1,0:T(1,128)}, u32[]{:S(2)}) copy-start(f32[1,256]{1,0:T(1,128)} %get-tuple-element.89) | copy-start | bytes 3076
  263.0 13.4 %copy-start.18 = (f32[1,256]{1,0:T(1,128)S(1)}, f32[1,256]{1,0:T(1,128)}, u32[]{:S(2)}) copy-start(f32[1,256]{1,0:T(1,128)} %get-tuple-element.90) | copy-start | bytes 3076
  263.0 13.4 %copy-start.19 = (f32[1,256]{1,0:T(1,128)S(1)}, f32[1,256]{1,0:T(1,128)}, u32[]{:S(2)}) copy-start(f32[1,256]{1,0:T(1,128)} %get-tuple-element.91) | copy-start | bytes 3076
  263.0 13.4 %copy-start.20 = (f32[1,256]{1,0:T(1,128)S(1)}, f32[1,256]{1,0:T(1,128)}, u32[]{:S(2)}) copy-start(f32[1,256]{1,0:T(1,128)} %get-tuple-element.92) | copy-start | bytes 3076
  263.1 13.4 %copy-start.21 = (f32[1,256]{1,0:T(1,128)S(1)}, f32[1,256]{1,0:T(1,128)}, u32[]{:S(2)}) copy-start(f32[1,256]{1,0:T(1,128)} %get-tuple-element.93) | copy-start | bytes 3076
Sparse Core Ops, SparseCore 0:
  278.0 47.9 reduce-scatter.3
where the time goes:
time: 341 us; the launch traced here: 335 us
  waiting for transfers between devices  116 us (34%)
  local copies, waits for them, and re-layouts  87.5 us (26%)
  other arithmetic  81.9 us (24%)
  between operations  32.6 us (10%)
  starting transfers between devices  15 us (4%)
    unnamed x2, waiting for transfers between devices  48.2 us
    ppermute x4, waiting for transfers between devices, with_halo(): lax.ppermute(lax.slice_in_dim(block, 0, width, axis=dim), axis, backward)  43.3 us
    slice x6, local copies, waits for them, and re-layouts, signature(): jnp.roll(centre, -1, 2) - 2.0 * centre + jnp.roll(centre, 1, 2)  39.4 us
    max x1, other arithmetic, per_device(): response = feature if response is None else jnp.maximum(response, feature)  31.9 us
    ppermute x4, waiting for transfers between devices, with_halo(): lax.ppermute(lax.slice_in_dim(block, block.shape[dim] - width, None, axis...  24.9 us
    gather x8, local copies, waits for them, and re-layouts, per_device(): summand = corner_weights[corner] * feature_table[:, cell_index]  21.4 us
    add x2, other arithmetic, smooth_periodic(): running = summand if running is None else running + summand  17.7 us
    ppermute x4, starting transfers between devices, with_halo(): lax.ppermute(lax.slice_in_dim(block, 0, width, axis=dim), axis, backward)  11.9 us
  transfers between devices with their start and end apart: 9, of which 7 were waited for; matrix products, arithmetic and copies ran while one was open for 11% of the time, Pallas kernels for 0%

commit v1 on v0

v1 whole, which is shorter than its diff:
```python
import functools

import jax
import jax.numpy as jnp
from jax import lax
from jax.experimental import pallas as pl
from jax.experimental.pallas import tpu as pltpu
from jax.sharding import PartitionSpec as P

SCALES = 3
HALO = 9
HOWN = 256
DMAX = 4
LANES = 128
TAPS = (0.375, 0.25, 0.0625)


def taps(centre, near, far, scale=1.0):
    return (TAPS[0] * scale) * centre + (TAPS[1] * scale) * near + (TAPS[2] * scale) * far


def kernel(depth, rows, width, bands, *refs):
    dil_ref, select_ref, xcell_ref, column_ref = refs[:4]
    parts = refs[4 : 4 + 3 * bands]
    resp_ref, cat_ref, field, along, smooth, feature, sems = refs[4 + 3 * bands :]
    tiles = width // LANES
    starts = (0, HALO, HALO + depth)
    copies = []
    for b in range(bands):
        for i in range(3):
            src = parts[3 * b + i]
            copies.append(
                pltpu.make_async_copy(
                    src,
                    field.at[pl.ds(starts[i], src.shape[0]), pl.ds(b * rows, rows)],
                    sems.at[3 * b + i],
                )
            )
    for copy in copies:
        copy.start()
    resp_ref[...] = jnp.full(resp_ref.shape, -jnp.inf, jnp.float32)
    for copy in copies:
        copy.wait()

    places = ((rows,), (0, 2 * rows)) if bands == 2 else ((rows,), (0,), (2 * rows,))
    lane = lax.broadcasted_iota(jnp.int32, (8, LANES), 1)
    groups = (rows + 2 + 7) // 8

    def level_body(level, carry):
        d = dil_ref[level]
        d2 = 2 * d

        def z_body(p, c):
            at = p + HALO - 1
            for b in range(bands):
                for r in range(0, rows, 8):
                    for x in range(0, width, 512):
                        def plane(k):
                            return field[at + k, b * rows + r : b * rows + r + 8, x : x + 512]

                        v = taps(plane(0), plane(d) + plane(-d), plane(d2) + plane(-d2))
                        for place in places[b]:
                            along[p, place + r : place + r + 8, x : x + 512] = v
            return c

        lax.fori_loop(0, depth + 2, z_body, 0)

        def xy_pass(d):
            d2 = 2 * d
            up1, up2 = lane < LANES - d, lane < LANES - d2
            dn1, dn2 = lane >= d, lane >= d2

            def xy_body(p, c):
                for g in range(groups):
                    base = rows - 1 + 8 * g

                    def row(k, j):
                        return along[p, base + k : base + k + 8, j * LANES : (j + 1) * LANES]

                    def prepare(j):
                        t = taps(row(0, j), row(d, j) + row(-d, j), row(d2, j) + row(-d2, j))
                        return (t,) + tuple(
                            pltpu.roll(t, shift, 1) for shift in (LANES - d, LANES - d2, d, d2)
                        )

                    ready = {j: prepare(j) for j in (tiles - 1, 0)}
                    for j in range(tiles):
                        n, m = (j + 1) % tiles, (j - 1) % tiles
                        if n not in ready:
                            ready[n] = prepare(n)
                        t, l1, l2, r1, r2 = ready[j]
                        near = jnp.where(up1, l1, ready[n][1]) + jnp.where(dn1, r1, ready[m][3])
                        far = jnp.where(up2, l2, ready[n][2]) + jnp.where(dn2, r2, ready[m][4])
                        smooth[p, 8 * g : 8 * g + 8, j * LANES : (j + 1) * LANES] = taps(
                            t, near, far, 4.0
                        )
                return c

            lax.fori_loop(0, depth + 2, xy_body, 0)

        for spacing in range(1, DMAX + 1):
            pl.when(d == spacing)(functools.partial(xy_pass, spacing))

        first, last = lane == 0, lane == LANES - 1

        def hess_body(z, c):
            for r in range(0, rows, 8):
                def at(dz, dy, j):
                    return smooth[
                        z + 1 + dz, r + 1 + dy : r + 9 + dy, j * LANES : (j + 1) * LANES
                    ]

                def prepare(j):
                    centre, zp, zm = at(0, 0, j), at(1, 0, j), at(-1, 0, j)
                    yp, ym = at(0, 1, j), at(0, -1, j)
                    twice = centre + centre
                    hzz = (zp + zm) - twice
                    hyy = (yp + ym) - twice
                    zy = (at(1, 1, j) - at(1, -1, j)) - (at(-1, 1, j) - at(-1, -1, j))
                    shifted = [
                        (pltpu.roll(v, LANES - 1, 1), pltpu.roll(v, 1, 1))
                        for v in (centre, zp - zm, yp - ym)
                    ]
                    return twice, hzz, hyy, zy, shifted

                def finish(j, low, mid, high):
                    twice, hzz, hyy, zy, shifted = mid
                    plus = [jnp.where(last, high[4][i][0], shifted[i][0]) for i in range(3)]
                    minus = [jnp.where(first, low[4][i][1], shifted[i][1]) for i in range(3)]
                    hxx = (plus[0] + minus[0]) - twice
                    zx = plus[1] - minus[1]
                    yx = plus[2] - minus[2]
                    flat = hxx + hyy
                    trace = flat + hzz
                    squares = 0.0625 * (zy * zy + zx * zx + yx * yx)
                    minors = hxx * hyy + flat * hzz - squares
                    value = (trace * trace * (1.0 / 3.0) - minors) / (1.0 + jnp.exp(trace))
                    lanes = slice(j * LANES, (j + 1) * LANES)
                    resp_ref[z, r : r + 8, lanes] = jnp.maximum(resp_ref[z, r : r + 8, lanes], value)
                    feature[pl.ds(pl.multiple_of(z * rows + r, 8), 8), lanes] = value

                ready = {j: prepare(j) for j in (tiles - 1, 0)}
                for j in range(tiles):
                    n = (j + 1) % tiles
                    if n not in ready:
                        ready[n] = prepare(n)
                    finish(j, ready[(j - 1) % tiles], ready[j], ready[n])
            return c

        lax.fori_loop(0, depth, hess_body, 0)

        xcell = xcell_ref[...]
        slots = xcell.shape[0]
        chunk = 512

        def gather_body(i, acc):
            x0 = pl.multiple_of(i * chunk, chunk)
            block = feature[:, pl.ds(x0, chunk)]
            where = lax.broadcasted_iota(jnp.int32, (slots, chunk), 1) + x0
            for dx in range(2):
                cell = xcell + dx
                cell = jnp.where(cell == width, 0, cell)
                picked = jnp.dot(
                    select_ref[dx],
                    block,
                    precision=lax.Precision.HIGHEST,
                    preferred_element_type=jnp.float32,
                )
                acc = acc + jnp.sum(jnp.where(where == cell, picked, 0.0), axis=1, keepdims=True)
            return acc

        partial = lax.fori_loop(0, width // chunk, gather_body, jnp.zeros((slots, 1), jnp.float32))
        column = lax.broadcasted_iota(jnp.int32, (slots, cat_ref.shape[2]), 1)
        spread = jnp.where(column == column_ref[...], partial, 0.0)
        cat_ref[level] = jnp.sum(spread, axis=0, keepdims=True)
        return carry

    lax.fori_loop(0, SCALES, level_body, 0)


def ring(axis, step):
    count = lax.axis_size(axis)
    return [(i, (i + step) % count) for i in range(count)]


def per_device(density, dilations, owner_rank, owner_slot, base_cell, corner_weights):
    depth, rows, width = density.shape
    groups = lax.axis_size("gy")

    def z_sides(block):
        low = lax.ppermute(block[depth - HALO :], "gz", ring("gz", 1))
        high = lax.ppermute(block[:HALO], "gz", ring("gz", -1))
        return [low, block, high]

    parts = z_sides(density)
    neighbours = [lax.ppermute(density, "gy", ring("gy", 1))]
    if groups != 2:
        neighbours.append(lax.ppermute(density, "gy", ring("gy", -1)))
    for band in neighbours:
        parts += z_sides(band)
    bands = 1 + len(neighbours)

    plane = (rows - 1) * width
    z_index = base_cell // plane
    remainder = base_cell % plane
    y_index = remainder // width
    x_index = remainder % width
    row_at = jnp.arange(depth * rows, dtype=jnp.int32)[None, :]
    select = []
    for step_x in (0, 1):
        chosen = 0.0
        for step_z in (0, 1):
            for step_y in (0, 1):
                row = (z_index + step_z) * rows + y_index + step_y
                weight = corner_weights[4 * step_z + 2 * step_y + step_x]
                chosen = chosen + jnp.where(row[:, None] == row_at, weight[:, None], 0.0)
        select.append(chosen)
    select = jnp.stack(select)
    column = owner_rank * HOWN + owner_slot[:, None]

    vmem = pl.BlockSpec(memory_space=pltpu.VMEM)
    cells = depth * rows * width
    response, spread = pl.pallas_call(
        functools.partial(kernel, depth, rows, width, bands),
        out_shape=(
            jax.ShapeDtypeStruct((depth, rows, width), jnp.float32),
            jax.ShapeDtypeStruct((SCALES, 1, groups * HOWN), jnp.float32),
        ),
        in_specs=[pl.BlockSpec(memory_space=pltpu.SMEM), vmem, vmem, vmem]
        + [pl.BlockSpec(memory_space=pl.ANY)] * (3 * bands),
        out_specs=(vmem, vmem),
        scratch_shapes=[
            pltpu.VMEM((depth + 2 * HALO, bands * rows, width), jnp.float32),
            pltpu.VMEM((depth + 2, 3 * rows, width), jnp.float32),
            pltpu.VMEM((depth + 2, (rows + 2 + 7) // 8 * 8, width), jnp.float32),
            pltpu.VMEM((depth * rows, width), jnp.float32),
            pltpu.SemaphoreType.DMA((3 * bands,)),
        ],
        compiler_params=pltpu.CompilerParams(vmem_limit_bytes=56 * 1024 * 1024),
        cost_estimate=pl.CostEstimate(
            flops=cells * SCALES * 100, bytes_accessed=cells * 4 * 8, transcendentals=cells * SCALES
        ),
    )(dilations, select, x_index[:, None], column, *parts)

    spread = spread[:, 0]
    me = lax.axis_index("gy")

    def share(owner):
        return lax.dynamic_slice_in_dim(spread, owner * HOWN, HOWN, axis=1)

    catalogue = share(me)
    for step in range(1, groups):
        catalogue = catalogue + lax.ppermute(
            share((me + step) % groups), "gy", ring("gy", step)
        )
    return (response, catalogue)


def solution(mesh):
    placed = (
        P("gz", "gy", None),
        P(),
        P(("gz", "gy"), None),
        P(("gz", "gy")),
        P(("gz", "gy")),
        P(None, ("gz", "gy")),
    )
    return jax.shard_map(
        per_device,
        mesh=mesh,
        in_specs=placed,
        out_specs=(P("gz", "gy", None), P(None, ("gz", "gy"))),
        check_vma=False,
    )
```

time: 341 us -> 112 us (0.33)
  the two profiles are of different devices: /device:TPU:0 before, /device:TPU:1 now
where the time goes in v1:
time: 112 us
  waiting for transfers between devices  50.1 us (45%)
  Pallas kernels  43.4 us (39%)
  starting transfers between devices  8 us (7%)
  local copies, waits for them, and re-layouts  7.46 us (7%)
  other arithmetic  1.93 us (2%)
    pallas_call x1, Pallas kernels, per_device(): pl.pallas_call(functools.partial(kernel, depth, rows, width, bands), out_...  43.4 us
    ppermute x1, waiting for transfers between devices, per_device(): neighbours = [lax.ppermute(density, 'gy', ring('gy', 1))]  23.3 us
    ppermute x2, waiting for transfers between devices, z_sides(): low = lax.ppermute(block[depth - HALO:], 'gz', ring('gz', 1))  23.1 us
    slice x2, local copies, waits for them, and re-layouts, z_sides(): high = lax.ppermute(block[:HALO], 'gz', ring('gz', -1))  5.11 us
    ppermute x2, starting transfers between devices, z_sides(): low = lax.ppermute(block[depth - HALO:], 'gz', ring('gz', 1))  4.68 us
    ppermute x2, waiting for transfers between devices, z_sides(): high = lax.ppermute(block[:HALO], 'gz', ring('gz', -1))  2.48 us
  transfers between devices with their start and end apart: 6, of which 4 were waited for; matrix products, arithmetic and copies ran while one was open for 7% of the time, Pallas kernels for 0%

profile of v1, /device:TPU:1, one launch (start us, length us, event | category | flops | bytes accessed | tf_op | source)
XLA Modules:
  0.0 111.6 jit_solution(15347369008136966833)
XLA Ops:
  0.6 2.1 %collective-permute-start.2 = (f32[10,16,2048]{2,1,0:T(8,128)}, f32[10,16,2048]{2,1,0:T(8,128)S(1)}, u32[]{:S(2)}, u32[]{:S(2)}) collective-permute-start(f32[10,16,2048]{2,1,0:T(8,128)} %refs_5_.1), channel_id=1, source_target_pairs={{0,1},{1,0},{2,3},{3,2},{4,5},{5,4},{6,7},{7,6},{8,9},{9,8},{10,11... | collective-permute-start | bytes 3932168 | tf_op jit(solution)/shard_map/ppermute | solution.py:196
  2.7 3.3 %fusion.1 = (f32[9,16,2048]{2,1,0:T(8,128)}, f32[9,16,2048]{2,1,0:T(8,128)}) fusion(f32[10,16,2048]{2,1,0:T(8,128)} %refs_5_.1), kind=kLoop, calls=%fused_computation.27 | loop fusion | bytes 4718592 | tf_op jit(solution)/shard_map/slice | solution.py:192
  6.0 2.1 %collective-permute-start = (f32[9,16,2048]{2,1,0:T(8,128)}, f32[9,16,2048]{2,1,0:T(8,128)S(1)}, u32[]{:S(2)}, u32[]{:S(2)}) collective-permute-start(f32[9,16,2048]{2,1,0:T(8,128)} %get-tuple-element.15), channel_id=1, source_target_pairs={{0,2},{2,4},{4,6},{6,8},{8,10},{10,12},{12,14},{14,16},{16,18},{18... | collective-permute-start | bytes 3538952 | tf_op jit(solution)/shard_map/ppermute | solution.py:191
  8.1 0.0 collective-permute-start.1
  8.1 0.0 copy-start.6
  8.1 0.0 copy-start.4
  8.1 0.0 copy-start.5
  8.1 0.0 copy-start.3
  8.1 23.3 %collective-permute-done.2.refs_8_ = f32[10,16,2048]{2,1,0:T(8,128)S(1)} collective-permute-done((f32[10,16,2048]{2,1,0:T(8,128)}, f32[10,16,2048]{2,1,0:T(8,128)S(1)}, u32[]{:S(2)}, u32[]{:S(2)}) %collective-permute-start.2) | collective-permute-done | bytes 1310752 | tf_op jit(solution)/shard_map/ppermute | solution.py:196
  31.5 0.0 copy-start
  31.5 1.8 %fusion = (f32[9,16,2048]{2,1,0:T(8,128)}, f32[9,16,2048]{2,1,0:T(8,128)}) fusion(f32[10,16,2048]{2,1,0:T(8,128)S(1)} %collective-permute-done.2.refs_8_), kind=kLoop, calls=%fused_computation.26 | loop fusion | bytes 4718592 | tf_op jit(solution)/shard_map/slice | solution.py:192
  33.3 0.0 copy-done
  33.3 2.6 %collective-permute-start.3 = (f32[9,16,2048]{2,1,0:T(8,128)}, f32[9,16,2048]{2,1,0:T(8,128)S(1)}, u32[]{:S(2)}, u32[]{:S(2)}) collective-permute-start(f32[9,16,2048]{2,1,0:T(8,128)} %get-tuple-element.13), channel_id=1, source_target_pairs={{0,2},{2,4},{4,6},{6,8},{8,10},{10,12},{12,14},{14,16},{16,18},{18... | collective-permute-start | bytes 3538952 | tf_op jit(solution)/shard_map/ppermute | solution.py:191
  35.9 0.0 collective-permute-start.4
  35.9 0.0 copy-done.6
  35.9 0.8 copy.14.refs_2_
  36.7 0.0 copy-done.4
  36.7 0.0 copy-done.5
  36.7 0.8 copy.15.refs_3_
  37.5 0.0 copy-done.3
  37.6 0.5 select_add_fusion.1
  38.0 0.8 pad_maximum_fusion.refs_1_
  38.9 0.0 collective-permute-done.refs_4_
  38.9 0.0 copy-start.1
  38.9 0.0 collective-permute-done.1.refs_6_
  38.9 23.1 %collective-permute-done.3.refs_7_ = f32[9,16,2048]{2,1,0:T(8,128)S(1)} collective-permute-done((f32[9,16,2048]{2,1,0:T(8,128)}, f32[9,16,2048]{2,1,0:T(8,128)S(1)}, u32[]{:S(2)}, u32[]{:S(2)}) %collective-permute-start.3) | collective-permute-done | bytes 1179680 | tf_op jit(solution)/shard_map/ppermute | solution.py:191
  62.0 0.0 copy-start.2
  62.0 2.5 %collective-permute-done.4.refs_9_ = f32[9,16,2048]{2,1,0:T(8,128)} collective-permute-done((f32[9,16,2048]{2,1,0:T(8,128)}, f32[9,16,2048]{2,1,0:T(8,128)}, u32[]{:S(2)}, u32[]{:S(2)}) %collective-permute-start.4) | collective-permute-done | bytes 1179680 | tf_op jit(solution)/shard_map/ppermute | solution.py:192
  64.5 0.0 copy-done.1
  64.5 0.0 copy-done.2
  64.5 43.4 %shard_map.77 = (f32[10,16,2048]{2,1,0:T(8,128)}, f32[3,1,512]{2,1,0:T(1,128)}) custom-call(s32[3]{0:T(128)} %refs_0_.1, f32[2,256,160]{2,1,0:T(8,128)} %pad_maximum_fusion.refs_1_, s32[256,1]{1,0:T(8,128)} %copy.14.refs_2_, s32[256,1]{1,0:T(8,128)} %copy.15.refs_3_, f32[9,16,2048]{2,1,0:T(8,128)} %copy-done.1, f32[10,16,2048]{2,1,0:T(8,128)} %refs_5_.1, ...), custom_call_target="tpu_custom_call" | custom-call | flops 98304000 | bytes 10485760 | tf_op jit(solution)/shard_map/pallas_call | solution.py:223
  107.8 0.7 constant_dynamic-slice_fusion.1
  108.5 1.2 %collective-permute-start.5 = (f32[3,256]{1,0:T(4,128)S(1)}, f32[3,256]{1,0:T(4,128)S(1)}, u32[]{:S(2)}, u32[]{:S(2)}) collective-permute-start(f32[3,256]{1,0:T(4,128)S(1)} %bitcast.24), channel_id=1, source_target_pairs={{0,1},{1,0},{2,3},{3,2},{4,5},{5,4},{6,7},{7,6},{8,9},{9,8},{10,11... | collective-permute-start | bytes 9224 | tf_op jit(solution)/shard_map/ppermute | solution.py:253
  109.7 1.2 %collective-permute-done.5 = f32[3,256]{1,0:T(4,128)S(1)} collective-permute-done((f32[3,256]{1,0:T(4,128)S(1)}, f32[3,256]{1,0:T(4,128)S(1)}, u32[]{:S(2)}, u32[]{:S(2)}) %collective-permute-start.5) | collective-permute-done | bytes 3104 | tf_op jit(solution)/shard_map/ppermute | solution.py:253
  111.0 0.6 bitcast_add_fusion
  (5 shorter events, 0.0 us)
Async XLA Ops:
  0.6 30.8 %collective-permute-start.2 = (f32[10,16,2048]{2,1,0:T(8,128)}, f32[10,16,2048]{2,1,0:T(8,128)S(1)}, u32[]{:S(2)}, u32[]{:S(2)}) collective-permute-start(f32[10,16,2048]{2,1,0:T(8,128)} %refs_5_.1), channel_id=1, source_target_pairs={{0,1},{1,0},{2,3},{3,2},{4,5},{5,4},{6,7},{7,6},{8,9},{9,8},{10,11... | collective-permute-start | bytes 3932168 | tf_op jit(solution)/shard_map/ppermute | solution.py:196
  6.0 32.8 %collective-permute-start = (f32[9,16,2048]{2,1,0:T(8,128)}, f32[9,16,2048]{2,1,0:T(8,128)S(1)}, u32[]{:S(2)}, u32[]{:S(2)}) collective-permute-start(f32[9,16,2048]{2,1,0:T(8,128)} %get-tuple-element.15), channel_id=1, source_target_pairs={{0,2},{2,4},{4,6},{6,8},{8,10},{10,12},{12,14},{14,16},{16,18},{18... | collective-permute-start | bytes 3538952 | tf_op jit(solution)/shard_map/ppermute | solution.py:191
  8.1 30.8 %collective-permute-start.1 = (f32[9,16,2048]{2,1,0:T(8,128)}, f32[9,16,2048]{2,1,0:T(8,128)}, u32[]{:S(2)}, u32[]{:S(2)}) collective-permute-start(f32[9,16,2048]{2,1,0:T(8,128)} %get-tuple-element.14), channel_id=1, source_target_pairs={{0,30},{2,0},{4,2},{6,4},{8,6},{10,8},{12,10},{14,12},{16,14},{18,... | collective-permute-start | bytes 3538952 | tf_op jit(solution)/shard_map/ppermute | solution.py:192
  8.1 27.8 %copy-start.6 = (s32[256]{0:T(256)S(1)}, s32[256]{0:T(256)}, u32[]{:S(2)}) copy-start(s32[256]{0:T(256)} %param.10) | copy-start | bytes 3076
  8.1 28.6 %copy-start.4 = (s32[256]{0:T(256)S(1)}, s32[256]{0:T(256)}, u32[]{:S(2)}) copy-start(s32[256]{0:T(256)} %param.9) | copy-start | bytes 3076
  8.1 28.6 %copy-start.5 = (s32[256,1]{0,1:T(1,128)S(1)}, s32[256,1]{0,1:T(1,128)}, u32[]{:S(2)}) copy-start(s32[256,1]{0,1:T(1,128)} %param.8) | copy-start | bytes 3076
  8.1 29.4 %copy-start.3 = (f32[8,256]{1,0:T(8,128)S(1)}, f32[8,256]{1,0:T(8,128)}, u32[]{:S(2)}) copy-start(f32[8,256]{1,0:T(8,128)} %param.11) | copy-start | bytes 24580
  31.5 1.8 %copy-start = (f32[10,16,2048]{2,1,0:T(8,128)}, f32[10,16,2048]{2,1,0:T(8,128)S(1)}, u32[]{:S(2)}) copy-start(f32[10,16,2048]{2,1,0:T(8,128)S(1)} %collective-permute-done.2.refs_8_) | copy-start | bytes 3932164
  33.3 28.7 %collective-permute-start.3 = (f32[9,16,2048]{2,1,0:T(8,128)}, f32[9,16,2048]{2,1,0:T(8,128)S(1)}, u32[]{:S(2)}, u32[]{:S(2)}) collective-permute-start(f32[9,16,2048]{2,1,0:T(8,128)} %get-tuple-element.13), channel_id=1, source_target_pairs={{0,2},{2,4},{4,6},{6,8},{8,10},{10,12},{12,14},{14,16},{16,18},{18... | collective-permute-start | bytes 3538952 | tf_op jit(solution)/shard_map/ppermute | solution.py:191
  35.9 28.6 %collective-permute-start.4 = (f32[9,16,2048]{2,1,0:T(8,128)}, f32[9,16,2048]{2,1,0:T(8,128)}, u32[]{:S(2)}, u32[]{:S(2)}) collective-permute-start(f32[9,16,2048]{2,1,0:T(8,128)} %get-tuple-element.12), channel_id=1, source_target_pairs={{0,30},{2,0},{4,2},{6,4},{8,6},{10,8},{12,10},{14,12},{16,14},{18,... | collective-permute-start | bytes 3538952 | tf_op jit(solution)/shard_map/ppermute | solution.py:192
  38.9 25.6 %copy-start.1 = (f32[9,16,2048]{2,1,0:T(8,128)}, f32[9,16,2048]{2,1,0:T(8,128)S(1)}, u32[]{:S(2)}) copy-start(f32[9,16,2048]{2,1,0:T(8,128)S(1)} %collective-permute-done.refs_4_) | copy-start | bytes 3538948
  62.0 2.5 %copy-start.2 = (f32[9,16,2048]{2,1,0:T(8,128)}, f32[9,16,2048]{2,1,0:T(8,128)S(1)}, u32[]{:S(2)}) copy-start(f32[9,16,2048]{2,1,0:T(8,128)S(1)} %collective-permute-done.3.refs_7_) | copy-start | bytes 3538948
  108.5 2.5 %collective-permute-start.5 = (f32[3,256]{1,0:T(4,128)S(1)}, f32[3,256]{1,0:T(4,128)S(1)}, u32[]{:S(2)}, u32[]{:S(2)}) collective-permute-start(f32[3,256]{1,0:T(4,128)S(1)} %bitcast.24), channel_id=1, source_target_pairs={{0,1},{1,0},{2,3},{3,2},{4,5},{5,4},{6,7},{7,6},{8,9},{9,8},{10,11... | collective-permute-start | bytes 9224 | tf_op jit(solution)/shard_map/ppermute | solution.py:253

commit v2 on v1

--- a/solution.py
+++ b/solution.py
@@ -19,26 +19,37 @@
     return (TAPS[0] * scale) * centre + (TAPS[1] * scale) * near + (TAPS[2] * scale) * far
 
 
-def kernel(depth, rows, width, bands, *refs):
+def kernel(depth, rows, bands, tiles, first_tile, width, pieces, aliased, *refs):
     dil_ref, select_ref, xcell_ref, column_ref = refs[:4]
-    parts = refs[4 : 4 + 3 * bands]
-    resp_ref, cat_ref, field, along, smooth, feature, sems = refs[4 + 3 * bands :]
-    tiles = width // LANES
+    count = 4 + 3 * bands * len(pieces)
+    parts = refs[4:count]
+    if aliased:
+        count += 1
+    out_ref, cat_ref, field, along, smooth, feature, chosen, resp, sems = refs[count:]
+    span = tiles * LANES
+    kept = span - 2 * LANES
     starts = (0, HALO, HALO + depth)
     copies = []
-    for b in range(bands):
-        for i in range(3):
-            src = parts[3 * b + i]
-            copies.append(
-                pltpu.make_async_copy(
-                    src,
-                    field.at[pl.ds(starts[i], src.shape[0]), pl.ds(b * rows, rows)],
-                    sems.at[3 * b + i],
+    for n, (low, size, to) in enumerate(pieces):
+        for b in range(bands):
+            for i in range(3):
+                src = parts[(n * bands + b) * 3 + i]
+                planes = depth if i == 1 else HALO
+                copies.append(
+                    pltpu.make_async_copy(
+                        src.at[:, :, pl.ds(low[src.shape[2] == width], size)],
+                        field.at[pl.ds(starts[i], planes), pl.ds(b * rows, rows), pl.ds(to, size)],
+                        sems.at[len(copies)],
+                    )
                 )
-            )
     for copy in copies:
         copy.start()
-    resp_ref[...] = jnp.full(resp_ref.shape, -jnp.inf, jnp.float32)
+    resp[...] = jnp.full(resp.shape, -jnp.inf, jnp.float32)
+    for dx in range(2):
+        weights = select_ref[dx]
+        high = weights.astype(jnp.bfloat16)
+        rest = (weights - high.astype(jnp.float32)).astype(jnp.bfloat16)
+        chosen[dx] = jnp.concatenate([high, high, rest], axis=1)
     for copy in copies:
         copy.wait()
 
@@ -54,7 +65,7 @@
             at = p + HALO - 1
             for b in range(bands):
                 for r in range(0, rows, 8):
-                    for x in range(0, width, 512):
+                    for x in range(0, span, 512):
                         def plane(k):
                             return field[at + k, b * rows + r : b * rows + r + 8, x : x + 512]
 
@@ -135,41 +146,39 @@
                     squares = 0.0625 * (zy * zy + zx * zx + yx * yx)
                     minors = hxx * hyy + flat * hzz - squares
                     value = (trace * trace * (1.0 / 3.0) - minors) / (1.0 + jnp.exp(trace))
-                    lanes = slice(j * LANES, (j + 1) * LANES)
-                    resp_ref[z, r : r + 8, lanes] = jnp.maximum(resp_ref[z, r : r + 8, lanes], value)
+                    lanes = slice((j - 1) * LANES, j * LANES)
+                    resp[z, r : r + 8, lanes] = jnp.maximum(resp[z, r : r + 8, lanes], value)
                     feature[pl.ds(pl.multiple_of(z * rows + r, 8), 8), lanes] = value
 
-                ready = {j: prepare(j) for j in (tiles - 1, 0)}
-                for j in range(tiles):
-                    n = (j + 1) % tiles
-                    if n not in ready:
-                        ready[n] = prepare(n)
-                    finish(j, ready[(j - 1) % tiles], ready[j], ready[n])
+                ready = [prepare(0), prepare(1)]
+                for j in range(1, tiles - 1):
+                    ready.append(prepare(j + 1))
+                    finish(j, *ready[j - 1 : j + 2])
             return c
 
         lax.fori_loop(0, depth, hess_body, 0)
 
         xcell = xcell_ref[...]
         slots = xcell.shape[0]
-        chunk = 512
+        chunk = 256
 
         def gather_body(i, acc):
             x0 = pl.multiple_of(i * chunk, chunk)
             block = feature[:, pl.ds(x0, chunk)]
+            high = block.astype(jnp.bfloat16)
+            rest = (block - high.astype(jnp.float32)).astype(jnp.bfloat16)
+            block = jnp.concatenate([high, rest, high], axis=0)
             where = lax.broadcasted_iota(jnp.int32, (slots, chunk), 1) + x0
+            where = where + (first_tile + 1) * LANES
+            where = jnp.where(where >= width, where - width, where)
             for dx in range(2):
                 cell = xcell + dx
                 cell = jnp.where(cell == width, 0, cell)
-                picked = jnp.dot(
-                    select_ref[dx],
-                    block,
-                    precision=lax.Precision.HIGHEST,
-                    preferred_element_type=jnp.float32,
-                )
+                picked = jnp.dot(chosen[dx], block, preferred_element_type=jnp.float32)
                 acc = acc + jnp.sum(jnp.where(where == cell, picked, 0.0), axis=1, keepdims=True)
             return acc
 
-        partial = lax.fori_loop(0, width // chunk, gather_body, jnp.zeros((slots, 1), jnp.float32))
+        partial = lax.fori_loop(0, kept // chunk, gather_body, jnp.zeros((slots, 1), jnp.float32))
         column = lax.broadcasted_iota(jnp.int32, (slots, cat_ref.shape[2]), 1)
         spread = jnp.where(column == column_ref[...], partial, 0.0)
         cat_ref[level] = jnp.sum(spread, axis=0, keepdims=True)
@@ -177,6 +186,21 @@
 
     lax.fori_loop(0, SCALES, level_body, 0)
 
+    until = min(kept, width - (first_tile + 1) * LANES)
+    outs = [(0, (first_tile + 1) * LANES, until)]
+    if until < kept:
+        outs.append((until, 0, kept - until))
+    copies = [
+        pltpu.make_async_copy(
+            resp.at[:, :, pl.ds(low, size)], out_ref.at[:, :, pl.ds(to, size)], sems.at[n]
+        )
+        for n, (low, to, size) in enumerate(outs)
+    ]
+    for copy in copies:
+        copy.start()
+    for copy in copies:
+        copy.wait()
+
 
 def ring(axis, step):
     count = lax.axis_size(axis)
@@ -187,18 +211,36 @@
     depth, rows, width = density.shape
     groups = lax.axis_size("gy")
 
+    half = width // 2
+
     def z_sides(block):
         low = lax.ppermute(block[depth - HALO :], "gz", ring("gz", 1))
         high = lax.ppermute(block[:HALO], "gz", ring("gz", -1))
-        return [low, block, high]
-
-    parts = z_sides(density)
-    neighbours = [lax.ppermute(density, "gy", ring("gy", 1))]
-    if groups != 2:
-        neighbours.append(lax.ppermute(density, "gy", ring("gy", -1)))
-    for band in neighbours:
-        parts += z_sides(band)
-    bands = 1 + len(neighbours)
+        return low, high
+
+    def y_sides(block):
+        sides = [lax.ppermute(block, "gy", ring("gy", 1))]
+        if groups != 2:
+            sides.append(lax.ppermute(block, "gy", ring("gy", -1)))
+        return sides
+
+    front = density[:, :, :half]
+    beside = y_sides(front)
+    low, high = z_sides(front)
+    beside, later = lax.optimization_barrier((beside, density))
+    parts_a = [low, density, high]
+    back = later[:, :, half:]
+    beside_b = y_sides(back)
+    for band in beside:
+        low, high = z_sides(band)
+        parts_a += [low, band, high]
+    low, high = z_sides(back)
+    parts_b = [low, density, high]
+    beside_b, parts_a = lax.optimization_barrier((beside_b, parts_a))
+    for band in beside_b:
+        low, high = z_sides(band)
+        parts_b += [low, band, high]
+    bands = 1 + len(beside)
 
     plane = (rows - 1) * width
     z_index = base_cell // plane
@@ -219,28 +261,59 @@
     column = owner_rank * HOWN + owner_slot[:, None]
 
     vmem = pl.BlockSpec(memory_space=pltpu.VMEM)
-    cells = depth * rows * width
-    response, spread = pl.pallas_call(
-        functools.partial(kernel, depth, rows, width, bands),
-        out_shape=(
-            jax.ShapeDtypeStruct((depth, rows, width), jnp.float32),
-            jax.ShapeDtypeStruct((SCALES, 1, groups * HOWN), jnp.float32),
-        ),
-        in_specs=[pl.BlockSpec(memory_space=pltpu.SMEM), vmem, vmem, vmem]
-        + [pl.BlockSpec(memory_space=pl.ANY)] * (3 * bands),
-        out_specs=(vmem, vmem),
-        scratch_shapes=[
-            pltpu.VMEM((depth + 2 * HALO, bands * rows, width), jnp.float32),
-            pltpu.VMEM((depth + 2, 3 * rows, width), jnp.float32),
-            pltpu.VMEM((depth + 2, (rows + 2 + 7) // 8 * 8, width), jnp.float32),
-            pltpu.VMEM((depth * rows, width), jnp.float32),
-            pltpu.SemaphoreType.DMA((3 * bands,)),
-        ],
-        compiler_params=pltpu.CompilerParams(vmem_limit_bytes=56 * 1024 * 1024),
-        cost_estimate=pl.CostEstimate(
-            flops=cells * SCALES * 100, bytes_accessed=cells * 4 * 8, transcendentals=cells * SCALES
-        ),
-    )(dilations, select, x_index[:, None], column, *parts)
+    anywhere = pl.BlockSpec(memory_space=pl.ANY)
+    half_tiles = half // LANES
+
+    def run(tiles, first_tile, pieces, parts, onto):
+        cells = depth * rows * tiles * LANES
+        operands = [dilations, select, x_index[:, None], column] + parts
+        in_specs = [pl.BlockSpec(memory_space=pltpu.SMEM), vmem, vmem, vmem]
+        in_specs += [anywhere] * len(parts)
+        aliases = {}
+        if onto is not None:
+            aliases = {len(operands): 0}
+            operands.append(onto)
+            in_specs.append(anywhere)
+        return pl.pallas_call(
+            functools.partial(
+                kernel, depth, rows, bands, tiles, first_tile, width, pieces, onto is not None
+            ),
+            out_shape=(
+                jax.ShapeDtypeStruct((depth, rows, width), jnp.float32),
+                jax.ShapeDtypeStruct((SCALES, 1, groups * HOWN), jnp.float32),
+            ),
+            in_specs=in_specs,
+            out_specs=(anywhere, vmem),
+            input_output_aliases=aliases,
+            scratch_shapes=[
+                pltpu.VMEM((depth + 2 * HALO, bands * rows, tiles * LANES), jnp.float32),
+                pltpu.VMEM((depth + 2, 3 * rows, tiles * LANES), jnp.float32),
+                pltpu.VMEM((depth + 2, (rows + 2 + 7) // 8 * 8, tiles * LANES), jnp.float32),
+                pltpu.VMEM((depth * rows, (tiles - 2) * LANES), jnp.float32),
+                pltpu.VMEM((2, base_cell.shape[0], 3 * depth * rows), jnp.bfloat16),
+                pltpu.VMEM((depth, rows, (tiles - 2) * LANES), jnp.float32),
+                pltpu.SemaphoreType.DMA((len(parts),)),
+            ],
+            compiler_params=pltpu.CompilerParams(vmem_limit_bytes=48 * 1024 * 1024),
+            cost_estimate=pl.CostEstimate(
+                flops=cells * SCALES * 100,
+                bytes_accessed=cells * 4 * 8,
+                transcendentals=cells * SCALES,
+            ),
+        )(*operands)
+
+    edge = 2 * LANES
+    pieces_a = (((0, 0), half, 0),)
+    pieces_b = (
+        ((half - edge, half - edge), edge, 0),
+        ((0, half), half, edge),
+        ((0, 0), edge, edge + half),
+    )
+    response, spread_a = run(half_tiles, 0, pieces_a, parts_a, None)
+    response, spread_b = run(
+        half_tiles + 4, half_tiles - 2, pieces_b, parts_a + parts_b + parts_a, response
+    )
+    spread = spread_a + spread_b
 
     spread = spread[:, 0]
     me = lax.axis_index("gy")

time: 112 us -> 98.9 us (0.88)
  the two profiles are of different devices: /device:TPU:1 before, /device:TPU:0 now
where the time goes in v2:
time: 98.9 us; the launch traced here: 98.7 us
  Pallas kernels  47.4 us (48%)
  starting transfers between devices  24.2 us (24%)
  waiting for transfers between devices  18.9 us (19%)
  local copies, waits for them, and re-layouts  6.28 us (6%)
  other arithmetic  1.14 us (1%)
    pallas_call x2, Pallas kernels, run(): pl.pallas_call(functools.partial(kernel, depth, rows, bands, tiles, first...  47.4 us
    ppermute x2, waiting for transfers between devices, y_sides(): sides = [lax.ppermute(block, 'gy', ring('gy', 1))]  16.3 us
    ppermute x4, starting transfers between devices, z_sides(): high = lax.ppermute(block[:HALO], 'gz', ring('gz', -1))  13.3 us
    ppermute x2, starting transfers between devices, y_sides(): sides = [lax.ppermute(block, 'gy', ring('gy', 1))]  4.74 us
    ppermute x4, starting transfers between devices, z_sides(): low = lax.ppermute(block[depth - HALO:], 'gz', ring('gz', 1))  4.55 us
    slice x4, local copies, waits for them, and re-layouts, z_sides(): high = lax.ppermute(block[:HALO], 'gz', ring('gz', -1))  3.82 us
    ppermute x1, waiting for transfers between devices, per_device(): lax.ppermute(share((me + step) % groups), 'gy', ring('gy', step))  2.13 us
  transfers between devices with their start and end apart: 11, of which 4 were waited for; matrix products, arithmetic and copies ran while one was open for 6% of the time, Pallas kernels for 20%

profile of v2, /device:TPU:0, one launch (start us, length us, event | category | flops | bytes accessed | tf_op | source)
XLA Modules:
  0.0 98.7 jit_solution(11092780691357325051)
XLA Ops:
  0.6 0.0 copy-start
  0.6 1.2 %slice.90 = f32[10,16,1024]{2,1,0:T(8,128)S(1)} slice(f32[10,16,2048]{2,1,0:T(8,128)} %refs_17_), slice={[0:10], [0:16], [0:1024]} | slice | bytes 1310720 | tf_op jit(solution)/shard_map/slice | solution.py:227
  1.9 0.0 copy-start.5
  1.9 3.0 %collective-permute-start = (f32[10,16,1024]{2,1,0:T(8,128)S(1)}, f32[10,16,1024]{2,1,0:T(8,128)S(1)}, u32[]{:S(2)}, u32[]{:S(2)}) collective-permute-start(f32[10,16,1024]{2,1,0:T(8,128)S(1)} %slice.90), channel_id=1, source_target_pairs={{0,1},{1,0},{2,3},{3,2},{4,5},{5,4},{6,7},{7,6},{8,9},{9,8},{10,11... | collective-permute-start | bytes 1966088 | tf_op jit(solution)/shard_map/ppermute | solution.py:222
  4.9 0.0 copy-done
  4.9 1.2 %fusion.1 = (f32[9,16,1024]{2,1,0:T(8,128)}, f32[9,16,1024]{2,1,0:T(8,128)}) fusion(f32[10,16,2048]{2,1,0:T(8,128)S(1)} %copy-done), kind=kLoop, calls=%fused_computation.27 | loop fusion | bytes 2359296 | tf_op jit(solution)/shard_map/slice | solution.py:218
  6.1 0.0 collective-permute-start.2
  6.1 4.4 %collective-permute-start.3 = (f32[9,16,1024]{2,1,0:T(8,128)}, f32[9,16,1024]{2,1,0:T(8,128)S(1)}, u32[]{:S(2)}, u32[]{:S(2)}) collective-permute-start(f32[9,16,1024]{2,1,0:T(8,128)} %get-tuple-element.36), channel_id=1, source_target_pairs={{0,30},{2,0},{4,2},{6,4},{8,6},{10,8},{12,10},{14,12},{16,14},{18,... | collective-permute-start | bytes 1769480 | tf_op jit(solution)/shard_map/ppermute | solution.py:218
  10.5 0.0 copy-done.5
  10.6 0.0 copy-start.3
  10.6 0.0 copy-start.4
  10.6 9.0 %collective-permute-done.refs_8_.refs_20_ = f32[10,16,1024]{2,1,0:T(8,128)S(1)} collective-permute-done((f32[10,16,1024]{2,1,0:T(8,128)S(1)}, f32[10,16,1024]{2,1,0:T(8,128)S(1)}, u32[]{:S(2)}, u32[]{:S(2)}) %collective-permute-start) | collective-permute-done | bytes 655392 | tf_op jit(solution)/shard_map/ppermute | solution.py:222
  19.6 1.1 %fusion.3 = (f32[9,16,1024]{2,1,0:T(8,128)}, f32[9,16,1024]{2,1,0:T(8,128)}) fusion(f32[10,16,1024]{2,1,0:T(8,128)S(1)} %collective-permute-done.refs_8_.refs_20_), kind=kLoop, calls=%fused_computation.29 | loop fusion | bytes 2359296 | tf_op jit(solution)/shard_map/slice | solution.py:218
  20.8 0.0 copy-start.2
  20.8 0.0 collective-permute-start.4
  20.8 4.4 %collective-permute-start.5 = (f32[9,16,1024]{2,1,0:T(8,128)}, f32[9,16,1024]{2,1,0:T(8,128)}, u32[]{:S(2)}, u32[]{:S(2)}) collective-permute-start(f32[9,16,1024]{2,1,0:T(8,128)} %get-tuple-element.40), channel_id=1, source_target_pairs={{0,30},{2,0},{4,2},{6,4},{8,6},{10,8},{12,10},{14,12},{16,14},{18,... | collective-permute-start | bytes 1769480 | tf_op jit(solution)/shard_map/ppermute | solution.py:218
  25.2 0.9 slice.91
  26.1 1.7 %collective-permute-start.1 = (f32[10,16,1024]{2,1,0:T(8,128)}, f32[10,16,1024]{2,1,0:T(8,128)}, u32[]{:S(2)}, u32[]{:S(2)}) collective-permute-start(f32[10,16,1024]{2,1,0:T(8,128)} %slice.91), channel_id=1, source_target_pairs={{0,1},{1,0},{2,3},{3,2},{4,5},{5,4},{6,7},{7,6},{8,9},{9,8},{10,11... | collective-permute-start | bytes 1966088 | tf_op jit(solution)/shard_map/ppermute | solution.py:222
  27.9 0.0 copy-done.3
  27.9 0.0 copy-done.4
  27.9 0.1 copy.18.refs_2_
  28.0 0.1 copy.19.refs_3_
  28.2 0.0 copy-done.2
  28.2 0.1 fusion
  28.3 0.0 collective-permute-done.2.refs_4_.refs_16_
  28.3 0.1 collective-permute-start.6
  28.4 0.0 collective-permute-done.3.refs_6_.refs_18_
  28.4 4.4 %collective-permute-start.7 = (f32[9,16,1024]{2,1,0:T(8,128)S(1)}, f32[9,16,1024]{2,1,0:T(8,128)S(1)}, u32[]{:S(2)}, u32[]{:S(2)}) collective-permute-start(f32[9,16,1024]{2,1,0:T(8,128)S(1)} %get-tuple-element.34), channel_id=1, source_target_pairs={{0,30},{2,0},{4,2},{6,4},{8,6},{10,8},{12,10},{14,12},{16,14},{18,... | collective-permute-start | bytes 1769480 | tf_op jit(solution)/shard_map/ppermute | solution.py:218
  32.8 0.4 collective-permute-done.4.refs_7_.refs_19_
  33.2 0.0 collective-permute-done.5.refs_9_.refs_21_
  33.2 7.3 %collective-permute-done.1.refs_14_ = f32[10,16,1024]{2,1,0:T(8,128)} collective-permute-done((f32[10,16,1024]{2,1,0:T(8,128)}, f32[10,16,1024]{2,1,0:T(8,128)}, u32[]{:S(2)}, u32[]{:S(2)}) %collective-permute-start.1) | collective-permute-done | bytes 655392 | tf_op jit(solution)/shard_map/ppermute | solution.py:222
  40.5 1.4 %fusion.2 = (f32[9,16,1024]{2,1,0:T(8,128)S(1)}, f32[9,16,1024]{2,1,0:T(8,128)S(1)}) fusion(f32[10,16,1024]{2,1,0:T(8,128)} %collective-permute-done.1.refs_14_), kind=kLoop, calls=%fused_computation.28 | loop fusion | bytes 2359296 | tf_op jit(solution)/shard_map/slice | solution.py:218
  41.9 0.0 copy-start.1
  41.9 4.5 %collective-permute-start.8 = (f32[9,16,1024]{2,1,0:T(8,128)S(1)}, f32[9,16,1024]{2,1,0:T(8,128)S(1)}, u32[]{:S(2)}, u32[]{:S(2)}) collective-permute-start(f32[9,16,1024]{2,1,0:T(8,128)S(1)} %get-tuple-element.39), channel_id=1, source_target_pairs={{0,2},{2,4},{4,6},{6,8},{8,10},{10,12},{12,14},{14,16},{16,18},{18... | collective-permute-start | bytes 1769480 | tf_op jit(solution)/shard_map/ppermute | solution.py:217
  46.4 0.0 collective-permute-start.9
  46.4 0.5 select_add_fusion.1
  46.9 0.0 copy-done.1
  46.9 19.8 %shard_map.77 = (f32[10,16,2048]{2,1,0:T(8,128)}, f32[3,1,512]{2,1,0:T(1,128)S(1)}) custom-call(s32[3]{0:T(128)S(1)} %copy-done.1, f32[2,256,160]{2,1,0:T(8,128)S(1)} %pad_maximum_fusion.refs_1_, s32[256,1]{1,0:T(8,128)S(1)} %copy.18.refs_2_, s32[256,1]{1,0:T(8,128)S(1)} %copy.19.refs_3_, f32[9,16,1024]{2,1,0:T(8,128)S(1)} %collective-permute-done.2.refs_4_.refs_16_, ...), custom_call_target="tpu_custom_call" | custom-call | flops 49152000 | bytes 5242880 | tf_op jit(solution)/shard_map/pallas_call | solution.py:277
  66.7 0.0 collective-permute-done.6.refs_10_
  66.7 0.0 collective-permute-done.7.refs_12_
  66.8 0.0 collective-permute-done.8.refs_13_
  66.8 0.0 collective-permute-done.9.refs_15_
  66.8 27.6 %shard_map.78 = (f32[10,16,2048]{2,1,0:T(8,128)}, f32[3,1,512]{2,1,0:T(1,128)S(1)}) custom-call(s32[3]{0:T(128)S(1)} %copy-done.1, f32[2,256,160]{2,1,0:T(8,128)S(1)} %pad_maximum_fusion.refs_1_, s32[256,1]{1,0:T(8,128)S(1)} %copy.18.refs_2_, s32[256,1]{1,0:T(8,128)S(1)} %copy.19.refs_3_, ...), custom_call_target="tpu_custom_call", output_to_operand_aliasing={{0}: (22, {})} | custom-call | flops 73728000 | bytes 7864320 | tf_op jit(solution)/shard_map/pallas_call | solution.py:277
  94.4 1.5 %collective-permute-start.10 = (f32[3,256]{1,0:T(4,128)S(1)}, f32[3,256]{1,0:T(4,128)S(1)}, u32[]{:S(2)}, u32[]{:S(2)}) collective-permute-start(f32[3,256]{1,0:T(4,128)S(1)} %bitcast.24), channel_id=1, source_target_pairs={{0,1},{1,0},{2,3},{3,2},{4,5},{5,4},{6,7},{7,6},{8,9},{9,8},{10,11... | collective-permute-start | bytes 9224 | tf_op jit(solution)/shard_map/ppermute | solution.py:326
  96.0 2.1 %collective-permute-done.10 = f32[3,256]{1,0:T(4,128)S(1)} collective-permute-done((f32[3,256]{1,0:T(4,128)S(1)}, f32[3,256]{1,0:T(4,128)S(1)}, u32[]{:S(2)}, u32[]{:S(2)}) %collective-permute-start.10) | collective-permute-done | bytes 3104 | tf_op jit(solution)/shard_map/ppermute | solution.py:326
  98.1 0.6 bitcast_add_fusion
  (8 shorter events, 0.1 us)
Async XLA Ops:
  0.6 4.3 %copy-start = (f32[10,16,2048]{2,1,0:T(8,128)S(1)}, f32[10,16,2048]{2,1,0:T(8,128)}, u32[]{:S(2)}) copy-start(f32[10,16,2048]{2,1,0:T(8,128)} %refs_17_) | copy-start | bytes 3932164
  1.9 8.7 %copy-start.5 = (s32[256]{0:T(256)S(1)}, s32[256]{0:T(256)}, u32[]{:S(2)}) copy-start(s32[256]{0:T(256)} %param.10) | copy-start | bytes 3076
  1.9 17.7 %collective-permute-start = (f32[10,16,1024]{2,1,0:T(8,128)S(1)}, f32[10,16,1024]{2,1,0:T(8,128)S(1)}, u32[]{:S(2)}, u32[]{:S(2)}) collective-permute-start(f32[10,16,1024]{2,1,0:T(8,128)S(1)} %slice.90), channel_id=1, source_target_pairs={{0,1},{1,0},{2,3},{3,2},{4,5},{5,4},{6,7},{7,6},{8,9},{9,8},{10,11... | collective-permute-start | bytes 1966088 | tf_op jit(solution)/shard_map/ppermute | solution.py:222
  6.1 22.2 %collective-permute-start.2 = (f32[9,16,1024]{2,1,0:T(8,128)}, f32[9,16,1024]{2,1,0:T(8,128)S(1)}, u32[]{:S(2)}, u32[]{:S(2)}) collective-permute-start(f32[9,16,1024]{2,1,0:T(8,128)} %get-tuple-element.37), channel_id=1, source_target_pairs={{0,2},{2,4},{4,6},{6,8},{8,10},{10,12},{12,14},{14,16},{16,18},{18... | collective-permute-start | bytes 1769480 | tf_op jit(solution)/shard_map/ppermute | solution.py:217
  6.1 22.3 %collective-permute-start.3 = (f32[9,16,1024]{2,1,0:T(8,128)}, f32[9,16,1024]{2,1,0:T(8,128)S(1)}, u32[]{:S(2)}, u32[]{:S(2)}) collective-permute-start(f32[9,16,1024]{2,1,0:T(8,128)} %get-tuple-element.36), channel_id=1, source_target_pairs={{0,30},{2,0},{4,2},{6,4},{8,6},{10,8},{12,10},{14,12},{16,14},{18,... | collective-permute-start | bytes 1769480 | tf_op jit(solution)/shard_map/ppermute | solution.py:218
  10.6 17.3 %copy-start.3 = (s32[256]{0:T(256)S(1)}, s32[256]{0:T(256)}, u32[]{:S(2)}) copy-start(s32[256]{0:T(256)} %param.9) | copy-start | bytes 3076
  10.6 17.3 %copy-start.4 = (s32[256,1]{0,1:T(1,128)S(1)}, s32[256,1]{0,1:T(1,128)}, u32[]{:S(2)}) copy-start(s32[256,1]{0,1:T(1,128)} %param.8) | copy-start | bytes 3076
  20.8 7.4 %copy-start.2 = (f32[8,256]{1,0:T(8,128)S(1)}, f32[8,256]{1,0:T(8,128)}, u32[]{:S(2)}) copy-start(f32[8,256]{1,0:T(8,128)} %param.11) | copy-start | bytes 24580
  20.8 12.4 %collective-permute-start.4 = (f32[9,16,1024]{2,1,0:T(8,128)}, f32[9,16,1024]{2,1,0:T(8,128)}, u32[]{:S(2)}, u32[]{:S(2)}) collective-permute-start(f32[9,16,1024]{2,1,0:T(8,128)} %get-tuple-element.41), channel_id=1, source_target_pairs={{0,2},{2,4},{4,6},{6,8},{8,10},{10,12},{12,14},{14,16},{16,18},{18... | collective-permute-start | bytes 1769480 | tf_op jit(solution)/shard_map/ppermute | solution.py:217
  20.8 12.4 %collective-permute-start.5 = (f32[9,16,1024]{2,1,0:T(8,128)}, f32[9,16,1024]{2,1,0:T(8,128)}, u32[]{:S(2)}, u32[]{:S(2)}) collective-permute-start(f32[9,16,1024]{2,1,0:T(8,128)} %get-tuple-element.40), channel_id=1, source_target_pairs={{0,30},{2,0},{4,2},{6,4},{8,6},{10,8},{12,10},{14,12},{16,14},{18,... | collective-permute-start | bytes 1769480 | tf_op jit(solution)/shard_map/ppermute | solution.py:218
  26.1 14.4 %collective-permute-start.1 = (f32[10,16,1024]{2,1,0:T(8,128)}, f32[10,16,1024]{2,1,0:T(8,128)}, u32[]{:S(2)}, u32[]{:S(2)}) collective-permute-start(f32[10,16,1024]{2,1,0:T(8,128)} %slice.91), channel_id=1, source_target_pairs={{0,1},{1,0},{2,3},{3,2},{4,5},{5,4},{6,7},{7,6},{8,9},{9,8},{10,11... | collective-permute-start | bytes 1966088 | tf_op jit(solution)/shard_map/ppermute | solution.py:222
  28.3 38.4 %collective-permute-start.6 = (f32[9,16,1024]{2,1,0:T(8,128)S(1)}, f32[9,16,1024]{2,1,0:T(8,128)S(1)}, u32[]{:S(2)}, u32[]{:S(2)}) collective-permute-start(f32[9,16,1024]{2,1,0:T(8,128)S(1)} %get-tuple-element.35), channel_id=1, source_target_pairs={{0,2},{2,4},{4,6},{6,8},{8,10},{10,12},{12,14},{14,16},{16,18},{18... | collective-permute-start | bytes 1769480 | tf_op jit(solution)/shard_map/ppermute | solution.py:217
  28.4 38.3 %collective-permute-start.7 = (f32[9,16,1024]{2,1,0:T(8,128)S(1)}, f32[9,16,1024]{2,1,0:T(8,128)S(1)}, u32[]{:S(2)}, u32[]{:S(2)}) collective-permute-start(f32[9,16,1024]{2,1,0:T(8,128)S(1)} %get-tuple-element.34), channel_id=1, source_target_pairs={{0,30},{2,0},{4,2},{6,4},{8,6},{10,8},{12,10},{14,12},{16,14},{18,... | collective-permute-start | bytes 1769480 | tf_op jit(solution)/shard_map/ppermute | solution.py:218
  41.9 5.0 %copy-start.1 = (s32[3]{0:T(128)S(1)}, s32[3]{0:T(128)}, u32[]{:S(2)}) copy-start(s32[3]{0:T(128)} %refs_0_.3) | copy-start | bytes 40
  41.9 24.9 %collective-permute-start.8 = (f32[9,16,1024]{2,1,0:T(8,128)S(1)}, f32[9,16,1024]{2,1,0:T(8,128)S(1)}, u32[]{:S(2)}, u32[]{:S(2)}) collective-permute-start(f32[9,16,1024]{2,1,0:T(8,128)S(1)} %get-tuple-element.39), channel_id=1, source_target_pairs={{0,2},{2,4},{4,6},{6,8},{8,10},{10,12},{12,14},{14,16},{16,18},{18... | collective-permute-start | bytes 1769480 | tf_op jit(solution)/shard_map/ppermute | solution.py:217
  46.4 20.4 %collective-permute-start.9 = (f32[9,16,1024]{2,1,0:T(8,128)S(1)}, f32[9,16,1024]{2,1,0:T(8,128)S(1)}, u32[]{:S(2)}, u32[]{:S(2)}) collective-permute-start(f32[9,16,1024]{2,1,0:T(8,128)S(1)} %get-tuple-element.38), channel_id=1, source_target_pairs={{0,30},{2,0},{4,2},{6,4},{8,6},{10,8},{12,10},{14,12},{16,14},{18,... | collective-permute-start | bytes 1769480 | tf_op jit(solution)/shard_map/ppermute | solution.py:218
  94.4 3.7 %collective-permute-start.10 = (f32[3,256]{1,0:T(4,128)S(1)}, f32[3,256]{1,0:T(4,128)S(1)}, u32[]{:S(2)}, u32[]{:S(2)}) collective-permute-start(f32[3,256]{1,0:T(4,128)S(1)} %bitcast.24), channel_id=1, source_target_pairs={{0,1},{1,0},{2,3},{3,2},{4,5},{5,4},{6,7},{7,6},{8,9},{9,8},{10,11... | collective-permute-start | bytes 9224 | tf_op jit(solution)/shard_map/ppermute | solution.py:326

commit v3 on v2

--- a/solution.py
+++ b/solution.py
@@ -55,7 +55,9 @@
 
     places = ((rows,), (0, 2 * rows)) if bands == 2 else ((rows,), (0,), (2 * rows,))
     lane = lax.broadcasted_iota(jnp.int32, (8, LANES), 1)
-    groups = (rows + 2 + 7) // 8
+    groups = rows // 8
+    sub = lax.broadcasted_iota(jnp.int32, (8, LANES), 0)
+    top, bottom = sub == 0, sub == 7
 
     def level_body(level, carry):
         d = dil_ref[level]
@@ -82,14 +84,20 @@
             dn1, dn2 = lane >= d, lane >= d2
 
             def xy_body(p, c):
-                for g in range(groups):
-                    base = rows - 1 + 8 * g
-
-                    def row(k, j):
-                        return along[p, base + k : base + k + 8, j * LANES : (j + 1) * LANES]
+                for g in range(groups + 1):
 
                     def prepare(j):
-                        t = taps(row(0, j), row(d, j) + row(-d, j), row(d2, j) + row(-d2, j))
+                        def along_y(base):
+                            def row(k):
+                                at = slice(base + k, base + k + 8)
+                                return along[p, at, j * LANES : (j + 1) * LANES]
+
+                            return taps(row(0), row(d) + row(-d), row(d2) + row(-d2))
+
+                        if g == groups:
+                            t = jnp.where(top, along_y(2 * rows), along_y(rows - 8))
+                        else:
+                            t = along_y(rows + 8 * g)
                         return (t,) + tuple(
                             pltpu.roll(t, shift, 1) for shift in (LANES - d, LANES - d2, d, d2)
                         )
@@ -102,9 +110,9 @@
                         t, l1, l2, r1, r2 = ready[j]
                         near = jnp.where(up1, l1, ready[n][1]) + jnp.where(dn1, r1, ready[m][3])
                         far = jnp.where(up2, l2, ready[n][2]) + jnp.where(dn2, r2, ready[m][4])
-                        smooth[p, 8 * g : 8 * g + 8, j * LANES : (j + 1) * LANES] = taps(
-                            t, near, far, 4.0
-                        )
+                        t = taps(t, near, far, 4.0)
+                        for r in (0, rows + 8) if g == groups else (8 + 8 * g,):
+                            smooth[p, r : r + 8, j * LANES : (j + 1) * LANES] = t
                 return c
 
             lax.fori_loop(0, depth + 2, xy_body, 0)
@@ -115,45 +123,56 @@
         first, last = lane == 0, lane == LANES - 1
 
         def hess_body(z, c):
-            for r in range(0, rows, 8):
-                def at(dz, dy, j):
-                    return smooth[
-                        z + 1 + dz, r + 1 + dy : r + 9 + dy, j * LANES : (j + 1) * LANES
-                    ]
-
-                def prepare(j):
-                    centre, zp, zm = at(0, 0, j), at(1, 0, j), at(-1, 0, j)
-                    yp, ym = at(0, 1, j), at(0, -1, j)
-                    twice = centre + centre
-                    hzz = (zp + zm) - twice
-                    hyy = (yp + ym) - twice
-                    zy = (at(1, 1, j) - at(1, -1, j)) - (at(-1, 1, j) - at(-1, -1, j))
+            def prepare(j):
+                def at(dz, g):
+                    return smooth[z + 1 + dz, 8 * g : 8 * g + 8, j * LANES : (j + 1) * LANES]
+
+                centre = [at(0, g) for g in range(groups + 2)]
+                above = [at(1, g) for g in range(groups + 2)]
+                below = [at(-1, g) for g in range(groups + 2)]
+                slope = [a - b for a, b in zip(above, below)]
+
+                def beside(v, g):
+                    up = pltpu.roll(jnp.where(top, v[g + 1], v[g]), 7, 0)
+                    down = pltpu.roll(jnp.where(bottom, v[g - 1], v[g]), 1, 0)
+                    return up, down
+
+                results = []
+                for g in range(1, groups + 1):
+                    up, down = beside(centre, g)
+                    slope_up, slope_down = beside(slope, g)
+                    twice = centre[g] + centre[g]
+                    hzz = (above[g] + below[g]) - twice
+                    hyy = (up + down) - twice
+                    zy = slope_up - slope_down
                     shifted = [
                         (pltpu.roll(v, LANES - 1, 1), pltpu.roll(v, 1, 1))
-                        for v in (centre, zp - zm, yp - ym)
+                        for v in (centre[g], slope[g], up - down)
                     ]
-                    return twice, hzz, hyy, zy, shifted
-
-                def finish(j, low, mid, high):
-                    twice, hzz, hyy, zy, shifted = mid
-                    plus = [jnp.where(last, high[4][i][0], shifted[i][0]) for i in range(3)]
-                    minus = [jnp.where(first, low[4][i][1], shifted[i][1]) for i in range(3)]
-                    hxx = (plus[0] + minus[0]) - twice
-                    zx = plus[1] - minus[1]
-                    yx = plus[2] - minus[2]
-                    flat = hxx + hyy
-                    trace = flat + hzz
-                    squares = 0.0625 * (zy * zy + zx * zx + yx * yx)
-                    minors = hxx * hyy + flat * hzz - squares
-                    value = (trace * trace * (1.0 / 3.0) - minors) / (1.0 + jnp.exp(trace))
-                    lanes = slice((j - 1) * LANES, j * LANES)
-                    resp[z, r : r + 8, lanes] = jnp.maximum(resp[z, r : r + 8, lanes], value)
-                    feature[pl.ds(pl.multiple_of(z * rows + r, 8), 8), lanes] = value
-
-                ready = [prepare(0), prepare(1)]
-                for j in range(1, tiles - 1):
-                    ready.append(prepare(j + 1))
-                    finish(j, *ready[j - 1 : j + 2])
+                    results.append((twice, hzz, hyy, zy, shifted))
+                return results
+
+            def finish(j, r, low, mid, high):
+                twice, hzz, hyy, zy, shifted = mid
+                plus = [jnp.where(last, high[4][i][0], shifted[i][0]) for i in range(3)]
+                minus = [jnp.where(first, low[4][i][1], shifted[i][1]) for i in range(3)]
+                hxx = (plus[0] + minus[0]) - twice
+                zx = plus[1] - minus[1]
+                yx = plus[2] - minus[2]
+                flat = hxx + hyy
+                trace = flat + hzz
+                squares = 0.0625 * (zy * zy + zx * zx + yx * yx)
+                minors = hxx * hyy + flat * hzz - squares
+                value = (trace * trace * (1.0 / 3.0) - minors) / (1.0 + jnp.exp(trace))
+                lanes = slice((j - 1) * LANES, j * LANES)
+                resp[z, r : r + 8, lanes] = jnp.maximum(resp[z, r : r + 8, lanes], value)
+                feature[pl.ds(pl.multiple_of(z * rows + r, 8), 8), lanes] = value
+
+            ready = [prepare(0), prepare(1)]
+            for j in range(1, tiles - 1):
+                ready.append(prepare(j + 1))
+                for g in range(groups):
+                    finish(j, 8 * g, *[ready[j + i][g] for i in (-1, 0, 1)])
             return c
 
         lax.fori_loop(0, depth, hess_body, 0)
@@ -227,9 +246,8 @@
     front = density[:, :, :half]
     beside = y_sides(front)
     low, high = z_sides(front)
-    beside, later = lax.optimization_barrier((beside, density))
+    beside, back = lax.optimization_barrier((beside, density[:, :, half:]))
     parts_a = [low, density, high]
-    back = later[:, :, half:]
     beside_b = y_sides(back)
     for band in beside:
         low, high = z_sides(band)
@@ -288,7 +306,7 @@
             scratch_shapes=[
                 pltpu.VMEM((depth + 2 * HALO, bands * rows, tiles * LANES), jnp.float32),
                 pltpu.VMEM((depth + 2, 3 * rows, tiles * LANES), jnp.float32),
-                pltpu.VMEM((depth + 2, (rows + 2 + 7) // 8 * 8, tiles * LANES), jnp.float32),
+                pltpu.VMEM((depth + 2, rows + 16, tiles * LANES), jnp.float32),
                 pltpu.VMEM((depth * rows, (tiles - 2) * LANES), jnp.float32),
                 pltpu.VMEM((2, base_cell.shape[0], 3 * depth * rows), jnp.bfloat16),
                 pltpu.VMEM((depth, rows, (tiles - 2) * LANES), jnp.float32),

time: 98.9 us -> 98.7 us (level)
  local copies, waits for them, and re-layouts: 6.28 us -> 7.79 us
  waiting for transfers between devices: 18.9 us -> 17.6 us
  Pallas kernels: 47.4 us -> 46.3 us
    slice x4, local copies, waits for them, and re-layouts: 3.82 us -> 5.12 us  [z_sides(): high = lax.ppermute(block[:HALO], 'gz', ring('gz', -1))]
    pallas_call x2, Pallas kernels: 47.4 us -> 46.3 us  [run(): pl.pallas_call(functools.partial(kernel, depth, rows, bands, tiles, first...]
    slice x2 -> x1, local copies, waits for them, and re-layouts: 2.12 us -> 2.34 us  [per_device(): beside, back = lax.optimization_barrier((beside, density[:, :, half:]))]
  transfers between devices with their start and end apart: 11 -> 11, of which waited for: 4 -> 3; matrix products, arithmetic and copies ran while one was open for 6% -> 6% of each run, Pallas kernels for 20% -> 20%
where the time goes in v3:
time: 98.7 us; the launch traced here: 98.6 us
  Pallas kernels  46.3 us (47%)
  starting transfers between devices  25 us (25%)
  waiting for transfers between devices  17.6 us (18%)
  local copies, waits for them, and re-layouts  7.79 us (8%)
  other arithmetic  1.14 us (1%)
    pallas_call x2, Pallas kernels, run(): pl.pallas_call(functools.partial(kernel, depth, rows, bands, tiles, first...  46.3 us
    ppermute x2, waiting for transfers between devices, y_sides(): sides = [lax.ppermute(block, 'gy', ring('gy', 1))]  15.4 us
    ppermute x4, starting transfers between devices, z_sides(): high = lax.ppermute(block[:HALO], 'gz', ring('gz', -1))  13.3 us
    ppermute x4, starting transfers between devices, z_sides(): low = lax.ppermute(block[depth - HALO:], 'gz', ring('gz', 1))  5.43 us
    slice x4, local copies, waits for them, and re-layouts, z_sides(): high = lax.ppermute(block[:HALO], 'gz', ring('gz', -1))  5.12 us
    ppermute x2, starting transfers between devices, y_sides(): sides = [lax.ppermute(block, 'gy', ring('gy', 1))]  4.68 us
    slice x1, local copies, waits for them, and re-layouts, per_device(): beside, back = lax.optimization_barrier((beside, density[:, :, half:]))  2.34 us
    ppermute x1, waiting for transfers between devices, per_device(): lax.ppermute(share((me + step) % groups), 'gy', ring('gy', step))  2.11 us
  transfers between devices with their start and end apart: 11, of which 3 were waited for; matrix products, arithmetic and copies ran while one was open for 6% of the time, Pallas kernels for 20%

profile of v3, /device:TPU:0, one launch (start us, length us, event | category | flops | bytes accessed | tf_op | source)
XLA Modules:
  0.0 98.6 jit_solution(3862670575501660969)
XLA Ops:
  0.6 0.0 copy-start
  0.6 2.3 %fusion.1 = (f32[10,16,1024]{2,1,0:T(8,128)}, f32[10,16,1024]{2,1,0:T(8,128)S(1)}) fusion(f32[10,16,2048]{2,1,0:T(8,128)} %refs_17_), kind=kLoop, calls=%fused_computation.27 | loop fusion | bytes 2621440 | tf_op jit(solution)/shard_map/slice | solution.py:249
  3.0 0.0 copy-start.5
  3.0 2.9 %collective-permute-start = (f32[10,16,1024]{2,1,0:T(8,128)S(1)}, f32[10,16,1024]{2,1,0:T(8,128)S(1)}, u32[]{:S(2)}, u32[]{:S(2)}) collective-permute-start(f32[10,16,1024]{2,1,0:T(8,128)S(1)} %get-tuple-element.37), channel_id=1, source_target_pairs={{0,1},{1,0},{2,3},{3,2},{4,5},{5,4},{6,7},{7,6},{8,9},{9,8},{10,11... | collective-permute-start | bytes 1966088 | tf_op jit(solution)/shard_map/ppermute | solution.py:241
  5.9 0.0 copy-done
  5.9 1.2 %fusion = (f32[9,16,1024]{2,1,0:T(8,128)}, f32[9,16,1024]{2,1,0:T(8,128)}) fusion(f32[10,16,2048]{2,1,0:T(8,128)S(1)} %copy-done), kind=kLoop, calls=%fused_computation.26 | loop fusion | bytes 2359296 | tf_op jit(solution)/shard_map/slice | solution.py:237
  7.1 0.0 copy-start.3
  7.1 0.0 copy-start.4
  7.1 0.0 collective-permute-start.2
  7.1 4.4 %collective-permute-start.3 = (f32[9,16,1024]{2,1,0:T(8,128)}, f32[9,16,1024]{2,1,0:T(8,128)S(1)}, u32[]{:S(2)}, u32[]{:S(2)}) collective-permute-start(f32[9,16,1024]{2,1,0:T(8,128)} %get-tuple-element.34), channel_id=1, source_target_pairs={{0,30},{2,0},{4,2},{6,4},{8,6},{10,8},{12,10},{14,12},{16,14},{18,... | collective-permute-start | bytes 1769480 | tf_op jit(solution)/shard_map/ppermute | solution.py:237
  11.6 0.0 copy-done.5
  11.6 9.1 %collective-permute-done.refs_8_.refs_20_ = f32[10,16,1024]{2,1,0:T(8,128)S(1)} collective-permute-done((f32[10,16,1024]{2,1,0:T(8,128)S(1)}, f32[10,16,1024]{2,1,0:T(8,128)S(1)}, u32[]{:S(2)}, u32[]{:S(2)}) %collective-permute-start) | collective-permute-done | bytes 655392 | tf_op jit(solution)/shard_map/ppermute | solution.py:241
  20.7 0.0 copy-start.2
  20.7 1.2 %fusion.4 = (f32[9,16,1024]{2,1,0:T(8,128)}, f32[9,16,1024]{2,1,0:T(8,128)}) fusion(f32[10,16,1024]{2,1,0:T(8,128)S(1)} %collective-permute-done.refs_8_.refs_20_), kind=kLoop, calls=%fused_computation.30 | loop fusion | bytes 2359296 | tf_op jit(solution)/shard_map/slice | solution.py:237
  21.8 0.0 collective-permute-start.4
  21.8 4.4 %collective-permute-start.5 = (f32[9,16,1024]{2,1,0:T(8,128)}, f32[9,16,1024]{2,1,0:T(8,128)}, u32[]{:S(2)}, u32[]{:S(2)}) collective-permute-start(f32[9,16,1024]{2,1,0:T(8,128)} %get-tuple-element.42), channel_id=1, source_target_pairs={{0,30},{2,0},{4,2},{6,4},{8,6},{10,8},{12,10},{14,12},{16,14},{18,... | collective-permute-start | bytes 1769480 | tf_op jit(solution)/shard_map/ppermute | solution.py:237
  26.3 1.7 %collective-permute-start.1 = (f32[10,16,1024]{2,1,0:T(8,128)}, f32[10,16,1024]{2,1,0:T(8,128)}, u32[]{:S(2)}, u32[]{:S(2)}) collective-permute-start(f32[10,16,1024]{2,1,0:T(8,128)} %get-tuple-element.15), channel_id=1, source_target_pairs={{0,1},{1,0},{2,3},{3,2},{4,5},{5,4},{6,7},{7,6},{8,9},{9,8},{10,11... | collective-permute-start | bytes 1966088 | tf_op jit(solution)/shard_map/ppermute | solution.py:241
  28.0 0.0 copy-done.3
  28.0 0.0 copy-done.4
  28.0 0.1 copy.18.refs_2_
  28.2 0.1 copy.19.refs_3_
  28.3 0.0 copy-done.2
  28.4 1.4 %fusion.3 = (f32[9,16,1024]{2,1,0:T(8,128)S(1)}, f32[9,16,1024]{2,1,0:T(8,128)S(1)}) fusion(f32[10,16,1024]{2,1,0:T(8,128)} %get-tuple-element.15), kind=kLoop, calls=%fused_computation.29 | loop fusion | bytes 2359296 | tf_op jit(solution)/shard_map/slice | solution.py:237
  29.8 0.0 collective-permute-done.2.refs_4_.refs_16_
  29.8 0.1 collective-permute-start.6
  29.8 0.0 collective-permute-done.3.refs_6_.refs_18_
  29.9 4.4 %collective-permute-start.7 = (f32[9,16,1024]{2,1,0:T(8,128)S(1)}, f32[9,16,1024]{2,1,0:T(8,128)S(1)}, u32[]{:S(2)}, u32[]{:S(2)}) collective-permute-start(f32[9,16,1024]{2,1,0:T(8,128)S(1)} %get-tuple-element.40), channel_id=1, source_target_pairs={{0,30},{2,0},{4,2},{6,4},{8,6},{10,8},{12,10},{14,12},{16,14},{18,... | collective-permute-start | bytes 1769480 | tf_op jit(solution)/shard_map/ppermute | solution.py:237
  34.3 0.0 collective-permute-done.4.refs_7_.refs_19_
  34.3 0.0 collective-permute-done.5.refs_9_.refs_21_
  34.3 6.4 %collective-permute-done.1.refs_14_ = f32[10,16,1024]{2,1,0:T(8,128)} collective-permute-done((f32[10,16,1024]{2,1,0:T(8,128)}, f32[10,16,1024]{2,1,0:T(8,128)}, u32[]{:S(2)}, u32[]{:S(2)}) %collective-permute-start.1) | collective-permute-done | bytes 655392 | tf_op jit(solution)/shard_map/ppermute | solution.py:241
  40.7 1.4 %fusion.2 = (f32[9,16,1024]{2,1,0:T(8,128)S(1)}, f32[9,16,1024]{2,1,0:T(8,128)S(1)}) fusion(f32[10,16,1024]{2,1,0:T(8,128)} %collective-permute-done.1.refs_14_), kind=kLoop, calls=%fused_computation.28 | loop fusion | bytes 2359296 | tf_op jit(solution)/shard_map/slice | solution.py:237
  42.0 0.0 copy-start.1
  42.0 5.4 %collective-permute-start.8 = (f32[9,16,1024]{2,1,0:T(8,128)S(1)}, f32[9,16,1024]{2,1,0:T(8,128)S(1)}, u32[]{:S(2)}, u32[]{:S(2)}) collective-permute-start(f32[9,16,1024]{2,1,0:T(8,128)S(1)} %get-tuple-element.39), channel_id=1, source_target_pairs={{0,2},{2,4},{4,6},{6,8},{8,10},{10,12},{12,14},{14,16},{16,18},{18... | collective-permute-start | bytes 1769480 | tf_op jit(solution)/shard_map/ppermute | solution.py:236
  47.4 0.0 collective-permute-start.9
  47.4 0.5 select_add_fusion.1
  47.9 0.0 copy-done.1
  47.9 19.6 %shard_map.77 = (f32[10,16,2048]{2,1,0:T(8,128)}, f32[3,1,512]{2,1,0:T(1,128)S(1)}) custom-call(s32[3]{0:T(128)S(1)} %copy-done.1, f32[2,256,160]{2,1,0:T(8,128)S(1)} %pad_maximum_fusion.refs_1_, s32[256,1]{1,0:T(8,128)S(1)} %copy.18.refs_2_, s32[256,1]{1,0:T(8,128)S(1)} %copy.19.refs_3_, f32[9,16,1024]{2,1,0:T(8,128)S(1)} %collective-permute-done.2.refs_4_.refs_16_, ...), custom_call_target="tpu_custom_call" | custom-call | flops 49152000 | bytes 5242880 | tf_op jit(solution)/shard_map/pallas_call | solution.py:295
  67.5 0.0 collective-permute-done.6.refs_10_
  67.5 0.0 collective-permute-done.7.refs_12_
  67.5 0.0 collective-permute-done.8.refs_13_
  67.5 0.0 collective-permute-done.9.refs_15_
  67.6 26.8 %shard_map.78 = (f32[10,16,2048]{2,1,0:T(8,128)}, f32[3,1,512]{2,1,0:T(1,128)S(1)}) custom-call(s32[3]{0:T(128)S(1)} %copy-done.1, f32[2,256,160]{2,1,0:T(8,128)S(1)} %pad_maximum_fusion.refs_1_, s32[256,1]{1,0:T(8,128)S(1)} %copy.18.refs_2_, s32[256,1]{1,0:T(8,128)S(1)} %copy.19.refs_3_, ...), custom_call_target="tpu_custom_call", output_to_operand_aliasing={{0}: (22, {})} | custom-call | flops 73728000 | bytes 7864320 | tf_op jit(solution)/shard_map/pallas_call | solution.py:295
  94.4 1.6 %collective-permute-start.10 = (f32[3,256]{1,0:T(4,128)S(1)}, f32[3,256]{1,0:T(4,128)S(1)}, u32[]{:S(2)}, u32[]{:S(2)}) collective-permute-start(f32[3,256]{1,0:T(4,128)S(1)} %bitcast.24), channel_id=1, source_target_pairs={{0,1},{1,0},{2,3},{3,2},{4,5},{5,4},{6,7},{7,6},{8,9},{9,8},{10,11... | collective-permute-start | bytes 9224 | tf_op jit(solution)/shard_map/ppermute | solution.py:344
  95.9 2.1 %collective-permute-done.10 = f32[3,256]{1,0:T(4,128)S(1)} collective-permute-done((f32[3,256]{1,0:T(4,128)S(1)}, f32[3,256]{1,0:T(4,128)S(1)}, u32[]{:S(2)}, u32[]{:S(2)}) %collective-permute-start.10) | collective-permute-done | bytes 3104 | tf_op jit(solution)/shard_map/ppermute | solution.py:344
  98.0 0.6 bitcast_add_fusion
  (8 shorter events, 0.1 us)
Async XLA Ops:
  0.6 5.3 %copy-start = (f32[10,16,2048]{2,1,0:T(8,128)S(1)}, f32[10,16,2048]{2,1,0:T(8,128)}, u32[]{:S(2)}) copy-start(f32[10,16,2048]{2,1,0:T(8,128)} %refs_17_) | copy-start | bytes 3932164
  3.0 8.6 %copy-start.5 = (s32[256]{0:T(256)S(1)}, s32[256]{0:T(256)}, u32[]{:S(2)}) copy-start(s32[256]{0:T(256)} %param.10) | copy-start | bytes 3076
  3.0 17.7 %collective-permute-start = (f32[10,16,1024]{2,1,0:T(8,128)S(1)}, f32[10,16,1024]{2,1,0:T(8,128)S(1)}, u32[]{:S(2)}, u32[]{:S(2)}) collective-permute-start(f32[10,16,1024]{2,1,0:T(8,128)S(1)} %get-tuple-element.37), channel_id=1, source_target_pairs={{0,1},{1,0},{2,3},{3,2},{4,5},{5,4},{6,7},{7,6},{8,9},{9,8},{10,11... | collective-permute-start | bytes 1966088 | tf_op jit(solution)/shard_map/ppermute | solution.py:241
  7.1 20.9 %copy-start.3 = (s32[256]{0:T(256)S(1)}, s32[256]{0:T(256)}, u32[]{:S(2)}) copy-start(s32[256]{0:T(256)} %param.9) | copy-start | bytes 3076
  7.1 20.9 %copy-start.4 = (s32[256,1]{0,1:T(1,128)S(1)}, s32[256,1]{0,1:T(1,128)}, u32[]{:S(2)}) copy-start(s32[256,1]{0,1:T(1,128)} %param.8) | copy-start | bytes 3076
  7.1 22.6 %collective-permute-start.2 = (f32[9,16,1024]{2,1,0:T(8,128)}, f32[9,16,1024]{2,1,0:T(8,128)S(1)}, u32[]{:S(2)}, u32[]{:S(2)}) collective-permute-start(f32[9,16,1024]{2,1,0:T(8,128)} %get-tuple-element.35), channel_id=1, source_target_pairs={{0,2},{2,4},{4,6},{6,8},{8,10},{10,12},{12,14},{14,16},{16,18},{18... | collective-permute-start | bytes 1769480 | tf_op jit(solution)/shard_map/ppermute | solution.py:236
  7.1 22.7 %collective-permute-start.3 = (f32[9,16,1024]{2,1,0:T(8,128)}, f32[9,16,1024]{2,1,0:T(8,128)S(1)}, u32[]{:S(2)}, u32[]{:S(2)}) collective-permute-start(f32[9,16,1024]{2,1,0:T(8,128)} %get-tuple-element.34), channel_id=1, source_target_pairs={{0,30},{2,0},{4,2},{6,4},{8,6},{10,8},{12,10},{14,12},{16,14},{18,... | collective-permute-start | bytes 1769480 | tf_op jit(solution)/shard_map/ppermute | solution.py:237
  20.7 7.7 %copy-start.2 = (f32[8,256]{1,0:T(8,128)S(1)}, f32[8,256]{1,0:T(8,128)}, u32[]{:S(2)}) copy-start(f32[8,256]{1,0:T(8,128)} %param.11) | copy-start | bytes 24580
  21.8 12.5 %collective-permute-start.4 = (f32[9,16,1024]{2,1,0:T(8,128)}, f32[9,16,1024]{2,1,0:T(8,128)}, u32[]{:S(2)}, u32[]{:S(2)}) collective-permute-start(f32[9,16,1024]{2,1,0:T(8,128)} %get-tuple-element.43), channel_id=1, source_target_pairs={{0,2},{2,4},{4,6},{6,8},{8,10},{10,12},{12,14},{14,16},{16,18},{18... | collective-permute-start | bytes 1769480 | tf_op jit(solution)/shard_map/ppermute | solution.py:236
  21.8 12.5 %collective-permute-start.5 = (f32[9,16,1024]{2,1,0:T(8,128)}, f32[9,16,1024]{2,1,0:T(8,128)}, u32[]{:S(2)}, u32[]{:S(2)}) collective-permute-start(f32[9,16,1024]{2,1,0:T(8,128)} %get-tuple-element.42), channel_id=1, source_target_pairs={{0,30},{2,0},{4,2},{6,4},{8,6},{10,8},{12,10},{14,12},{16,14},{18,... | collective-permute-start | bytes 1769480 | tf_op jit(solution)/shard_map/ppermute | solution.py:237
  26.3 14.4 %collective-permute-start.1 = (f32[10,16,1024]{2,1,0:T(8,128)}, f32[10,16,1024]{2,1,0:T(8,128)}, u32[]{:S(2)}, u32[]{:S(2)}) collective-permute-start(f32[10,16,1024]{2,1,0:T(8,128)} %get-tuple-element.15), channel_id=1, source_target_pairs={{0,1},{1,0},{2,3},{3,2},{4,5},{5,4},{6,7},{7,6},{8,9},{9,8},{10,11... | collective-permute-start | bytes 1966088 | tf_op jit(solution)/shard_map/ppermute | solution.py:241
  29.8 37.7 %collective-permute-start.6 = (f32[9,16,1024]{2,1,0:T(8,128)S(1)}, f32[9,16,1024]{2,1,0:T(8,128)S(1)}, u32[]{:S(2)}, u32[]{:S(2)}) collective-permute-start(f32[9,16,1024]{2,1,0:T(8,128)S(1)} %get-tuple-element.41), channel_id=1, source_target_pairs={{0,2},{2,4},{4,6},{6,8},{8,10},{10,12},{12,14},{14,16},{16,18},{18... | collective-permute-start | bytes 1769480 | tf_op jit(solution)/shard_map/ppermute | solution.py:236
  29.9 37.7 %collective-permute-start.7 = (f32[9,16,1024]{2,1,0:T(8,128)S(1)}, f32[9,16,1024]{2,1,0:T(8,128)S(1)}, u32[]{:S(2)}, u32[]{:S(2)}) collective-permute-start(f32[9,16,1024]{2,1,0:T(8,128)S(1)} %get-tuple-element.40), channel_id=1, source_target_pairs={{0,30},{2,0},{4,2},{6,4},{8,6},{10,8},{12,10},{14,12},{16,14},{18,... | collective-permute-start | bytes 1769480 | tf_op jit(solution)/shard_map/ppermute | solution.py:237
  42.0 5.9 %copy-start.1 = (s32[3]{0:T(128)S(1)}, s32[3]{0:T(128)}, u32[]{:S(2)}) copy-start(s32[3]{0:T(128)} %refs_0_.3) | copy-start | bytes 40
  42.0 25.5 %collective-permute-start.8 = (f32[9,16,1024]{2,1,0:T(8,128)S(1)}, f32[9,16,1024]{2,1,0:T(8,128)S(1)}, u32[]{:S(2)}, u32[]{:S(2)}) collective-permute-start(f32[9,16,1024]{2,1,0:T(8,128)S(1)} %get-tuple-element.39), channel_id=1, source_target_pairs={{0,2},{2,4},{4,6},{6,8},{8,10},{10,12},{12,14},{14,16},{16,18},{18... | collective-permute-start | bytes 1769480 | tf_op jit(solution)/shard_map/ppermute | solution.py:236
  47.4 20.1 %collective-permute-start.9 = (f32[9,16,1024]{2,1,0:T(8,128)S(1)}, f32[9,16,1024]{2,1,0:T(8,128)S(1)}, u32[]{:S(2)}, u32[]{:S(2)}) collective-permute-start(f32[9,16,1024]{2,1,0:T(8,128)S(1)} %get-tuple-element.38), channel_id=1, source_target_pairs={{0,30},{2,0},{4,2},{6,4},{8,6},{10,8},{12,10},{14,12},{16,14},{18,... | collective-permute-start | bytes 1769480 | tf_op jit(solution)/shard_map/ppermute | solution.py:237
  94.4 3.7 %collective-permute-start.10 = (f32[3,256]{1,0:T(4,128)S(1)}, f32[3,256]{1,0:T(4,128)S(1)}, u32[]{:S(2)}, u32[]{:S(2)}) collective-permute-start(f32[3,256]{1,0:T(4,128)S(1)} %bitcast.24), channel_id=1, source_target_pairs={{0,1},{1,0},{2,3},{3,2},{4,5},{5,4},{6,7},{7,6},{8,9},{9,8},{10,11... | collective-permute-start | bytes 9224 | tf_op jit(solution)/shard_map/ppermute | solution.py:344

commit v4 on v3

--- a/solution.py
+++ b/solution.py
@@ -49,7 +49,8 @@
         weights = select_ref[dx]
         high = weights.astype(jnp.bfloat16)
         rest = (weights - high.astype(jnp.float32)).astype(jnp.bfloat16)
-        chosen[dx] = jnp.concatenate([high, high, rest], axis=1)
+        slots = weights.shape[0]
+        chosen[dx * slots : (dx + 1) * slots] = jnp.concatenate([high, high, rest], axis=1)
     for copy in copies:
         copy.wait()
 
@@ -190,11 +191,14 @@
             where = lax.broadcasted_iota(jnp.int32, (slots, chunk), 1) + x0
             where = where + (first_tile + 1) * LANES
             where = jnp.where(where >= width, where - width, where)
+            picked = jnp.dot(chosen[...], block, preferred_element_type=jnp.float32)
+            kept_cells = 0.0
             for dx in range(2):
                 cell = xcell + dx
                 cell = jnp.where(cell == width, 0, cell)
-                picked = jnp.dot(chosen[dx], block, preferred_element_type=jnp.float32)
-                acc = acc + jnp.sum(jnp.where(where == cell, picked, 0.0), axis=1, keepdims=True)
+                corner = picked[dx * slots : (dx + 1) * slots]
+                kept_cells = kept_cells + jnp.where(where == cell, corner, 0.0)
+            acc = acc + jnp.sum(kept_cells, axis=1, keepdims=True)
             return acc
 
         partial = lax.fori_loop(0, kept // chunk, gather_body, jnp.zeros((slots, 1), jnp.float32))
@@ -248,15 +252,24 @@
     low, high = z_sides(front)
     beside, back = lax.optimization_barrier((beside, density[:, :, half:]))
     parts_a = [low, density, high]
-    beside_b = y_sides(back)
     for band in beside:
         low, high = z_sides(band)
         parts_a += [low, band, high]
+
+    def across(block, step_z, step_y):
+        slabs = lax.axis_size("gz")
+        pairs = [
+            (z * groups + y, (z + step_z) % slabs * groups + (y + step_y) % groups)
+            for z in range(slabs)
+            for y in range(groups)
+        ]
+        return lax.ppermute(block, ("gz", "gy"), pairs)
+
+    last_planes, first_planes = back[depth - HALO :], back[:HALO]
     low, high = z_sides(back)
     parts_b = [low, density, high]
-    beside_b, parts_a = lax.optimization_barrier((beside_b, parts_a))
-    for band in beside_b:
-        low, high = z_sides(band)
+    for band, step in zip(y_sides(back), (1, -1)):
+        low, high = across(last_planes, 1, step), across(first_planes, -1, step)
         parts_b += [low, band, high]
     bands = 1 + len(beside)
 
@@ -308,7 +321,7 @@
                 pltpu.VMEM((depth + 2, 3 * rows, tiles * LANES), jnp.float32),
                 pltpu.VMEM((depth + 2, rows + 16, tiles * LANES), jnp.float32),
                 pltpu.VMEM((depth * rows, (tiles - 2) * LANES), jnp.float32),
-                pltpu.VMEM((2, base_cell.shape[0], 3 * depth * rows), jnp.bfloat16),
+                pltpu.VMEM((2 * base_cell.shape[0], 3 * depth * rows), jnp.bfloat16),
                 pltpu.VMEM((depth, rows, (tiles - 2) * LANES), jnp.float32),
                 pltpu.SemaphoreType.DMA((len(parts),)),
             ],

time: 98.7 us -> 107 us (1.084)
  starting transfers between devices: 25 us -> 35 us
  waiting for transfers between devices: 17.6 us -> 16.4 us
    ppermute x0 -> x2, starting transfers between devices: none -> 20.6 us  [across(): return lax.ppermute(block, ('gz', 'gy'), pairs)]
    ppermute x2, waiting for transfers between devices: 15.4 us -> 9.07 us  [y_sides(): sides = [lax.ppermute(block, 'gy', ring('gy', 1))]]
    ppermute x4 -> x3, starting transfers between devices: 5.43 us -> 0.06 us  [z_sides(): low = lax.ppermute(block[depth - HALO:], 'gz', ring('gz', 1))]
    ppermute x4 -> x3, starting transfers between devices: 13.3 us -> 8.96 us  [z_sides(): high = lax.ppermute(block[:HALO], 'gz', ring('gz', -1))]
    ppermute x4 -> x3, waiting for transfers between devices: 0.01 us -> 4.34 us  [z_sides(): low = lax.ppermute(block[depth - HALO:], 'gz', ring('gz', 1))]
    slice x4 -> x3, local copies, waits for them, and re-layouts: 5.12 us -> 3.67 us  [z_sides(): high = lax.ppermute(block[:HALO], 'gz', ring('gz', -1))]
  transfers between devices with their start and end apart: 11 -> 11, of which waited for: 3 -> 3; matrix products, arithmetic and copies ran while one was open for 6% -> 4% of each run, Pallas kernels for 20% -> 18%
where the time goes in v4:
time: 107 us
  Pallas kernels  46.1 us (43%)
  starting transfers between devices  35 us (33%)
  waiting for transfers between devices  16.4 us (15%)
  local copies, waits for them, and re-layouts  7.19 us (7%)
  other arithmetic  1.14 us (1%)
    pallas_call x2, Pallas kernels, run(): pl.pallas_call(functools.partial(kernel, depth, rows, bands, tiles, first...  46.1 us
    ppermute x2, starting transfers between devices, across(): return lax.ppermute(block, ('gz', 'gy'), pairs)  20.6 us
    ppermute x2, waiting for transfers between devices, y_sides(): sides = [lax.ppermute(block, 'gy', ring('gy', 1))]  9.07 us
    ppermute x3, starting transfers between devices, z_sides(): high = lax.ppermute(block[:HALO], 'gz', ring('gz', -1))  8.96 us
    ppermute x2, starting transfers between devices, y_sides(): sides = [lax.ppermute(block, 'gy', ring('gy', 1))]  4.75 us
    ppermute x3, waiting for transfers between devices, z_sides(): low = lax.ppermute(block[depth - HALO:], 'gz', ring('gz', 1))  4.34 us
    slice x3, local copies, waits for them, and re-layouts, z_sides(): high = lax.ppermute(block[:HALO], 'gz', ring('gz', -1))  3.67 us
    ppermute x1, waiting for transfers between devices, per_device(): lax.ppermute(share((me + step) % groups), 'gy', ring('gy', step))  3.02 us
  transfers between devices with their start and end apart: 11, of which 3 were waited for; matrix products, arithmetic and copies ran while one was open for 4% of the time, Pallas kernels for 18%

profile of v4, /device:TPU:0, one launch (start us, length us, event | category | flops | bytes accessed | tf_op | source)
XLA Modules:
  0.0 106.8 jit_solution(17503935742740861900)
XLA Ops:
  0.6 0.0 copy-start
  0.6 2.4 %fusion = (f32[10,16,1024]{2,1,0:T(8,128)}, f32[10,16,1024]{2,1,0:T(8,128)S(1)}) fusion(f32[10,16,2048]{2,1,0:T(8,128)} %refs_17_.1), kind=kLoop, calls=%fused_computation.26 | loop fusion | bytes 2621440 | tf_op jit(solution)/shard_map/slice | solution.py:253
  3.0 0.0 copy-start.6
  3.0 2.9 %collective-permute-start.2 = (f32[10,16,1024]{2,1,0:T(8,128)S(1)}, f32[10,16,1024]{2,1,0:T(8,128)S(1)}, u32[]{:S(2)}, u32[]{:S(2)}) collective-permute-start(f32[10,16,1024]{2,1,0:T(8,128)S(1)} %get-tuple-element.21), channel_id=1, source_target_pairs={{0,1},{1,0},{2,3},{3,2},{4,5},{5,4},{6,7},{7,6},{8,9},{9,8},{10,11... | collective-permute-start | bytes 1966088 | tf_op jit(solution)/shard_map/ppermute | solution.py:245
  5.9 0.0 copy-done
  5.9 1.2 %fusion.1 = (f32[9,16,1024]{2,1,0:T(8,128)}, f32[9,16,1024]{2,1,0:T(8,128)}) fusion(f32[10,16,2048]{2,1,0:T(8,128)S(1)} %copy-done), kind=kLoop, calls=%fused_computation.27 | loop fusion | bytes 2359296 | tf_op jit(solution)/shard_map/slice | solution.py:241
  7.1 0.0 copy-start.4
  7.1 0.0 copy-start.5
  7.1 0.0 collective-permute-start
  7.1 4.4 %collective-permute-start.1 = (f32[9,16,1024]{2,1,0:T(8,128)}, f32[9,16,1024]{2,1,0:T(8,128)S(1)}, u32[]{:S(2)}, u32[]{:S(2)}) collective-permute-start(f32[9,16,1024]{2,1,0:T(8,128)} %get-tuple-element.22), channel_id=1, source_target_pairs={{0,30},{2,0},{4,2},{6,4},{8,6},{10,8},{12,10},{14,12},{16,14},{18,... | collective-permute-start | bytes 1769480 | tf_op jit(solution)/shard_map/ppermute | solution.py:241
  11.6 0.0 copy-done.6
  11.6 9.1 %collective-permute-done.2.refs_8_.refs_20_ = f32[10,16,1024]{2,1,0:T(8,128)S(1)} collective-permute-done((f32[10,16,1024]{2,1,0:T(8,128)S(1)}, f32[10,16,1024]{2,1,0:T(8,128)S(1)}, u32[]{:S(2)}, u32[]{:S(2)}) %collective-permute-start.2) | collective-permute-done | bytes 655392 | tf_op jit(solution)/shard_map/ppermute | solution.py:245
  20.7 0.0 copy-start.3
  20.7 1.2 %fusion.3 = (f32[9,16,1024]{2,1,0:T(8,128)}, f32[9,16,1024]{2,1,0:T(8,128)}) fusion(f32[10,16,1024]{2,1,0:T(8,128)S(1)} %collective-permute-done.2.refs_8_.refs_20_), kind=kLoop, calls=%fused_computation.29 | loop fusion | bytes 2359296 | tf_op jit(solution)/shard_map/slice | solution.py:241
  21.8 0.0 collective-permute-start.3
  21.8 4.4 %collective-permute-start.4 = (f32[9,16,1024]{2,1,0:T(8,128)}, f32[9,16,1024]{2,1,0:T(8,128)}, u32[]{:S(2)}, u32[]{:S(2)}) collective-permute-start(f32[9,16,1024]{2,1,0:T(8,128)} %get-tuple-element.26), channel_id=1, source_target_pairs={{0,30},{2,0},{4,2},{6,4},{8,6},{10,8},{12,10},{14,12},{16,14},{18,... | collective-permute-start | bytes 1769480 | tf_op jit(solution)/shard_map/ppermute | solution.py:241
  26.3 0.0 copy-done.4
  26.3 0.0 copy-done.5
  26.3 0.1 copy.18.refs_2_
  26.5 0.1 copy.19.refs_3_
  26.6 0.0 copy-done.3
  26.6 1.8 %collective-permute-start.8 = (f32[10,16,1024]{2,1,0:T(8,128)}, f32[10,16,1024]{2,1,0:T(8,128)S(1)}, u32[]{:S(2)}, u32[]{:S(2)}) collective-permute-start(f32[10,16,1024]{2,1,0:T(8,128)} %get-tuple-element.9), channel_id=1, source_target_pairs={{0,1},{1,0},{2,3},{3,2},{4,5},{5,4},{6,7},{7,6},{8,9},{9,8},{10,11... | collective-permute-start | bytes 1966088 | tf_op jit(solution)/shard_map/ppermute | solution.py:245
  28.4 1.3 %fusion.2 = (f32[9,16,1024]{2,1,0:T(8,128)S(1)}, f32[9,16,1024]{2,1,0:T(8,128)S(1)}) fusion(f32[10,16,1024]{2,1,0:T(8,128)} %get-tuple-element.9), kind=kLoop, calls=%fused_computation.28 | loop fusion | bytes 2359296 | tf_op jit(solution)/shard_map/slice | solution.py:241
  29.8 0.0 copy-start.1
  29.8 0.0 collective-permute-done.refs_4_.refs_16_
  29.8 0.1 collective-permute-start.5
  29.9 0.0 collective-permute-done.1.refs_6_.refs_18_
  29.9 0.1 collective-permute-start.7
  29.9 4.3 %collective-permute-done.3.refs_7_.refs_19_ = f32[9,16,1024]{2,1,0:T(8,128)} collective-permute-done((f32[9,16,1024]{2,1,0:T(8,128)}, f32[9,16,1024]{2,1,0:T(8,128)}, u32[]{:S(2)}, u32[]{:S(2)}) %collective-permute-start.3) | collective-permute-done | bytes 589856 | tf_op jit(solution)/shard_map/ppermute | solution.py:240
  34.3 0.1 collective-permute-start.6
  34.3 0.0 collective-permute-done.4.refs_9_.refs_21_
  34.3 20.5 %collective-permute-start.9 = (f32[9,16,1024]{2,1,0:T(8,128)S(1)}, f32[9,16,1024]{2,1,0:T(8,128)S(1)}, u32[]{:S(2)}, u32[]{:S(2)}) collective-permute-start(f32[9,16,1024]{2,1,0:T(8,128)S(1)} %get-tuple-element.24), channel_id=1, source_target_pairs={{0,31},{1,30},{2,1},{3,0},{4,3},{5,2},{6,5},{7,4},{8,7},{9,6},{10,... | collective-permute-start | bytes 1769480 | tf_op jit(solution)/shard_map/ppermute | solution.py:266
  54.9 0.5 select_add_fusion.1
  55.4 0.0 copy-done.1
  55.4 19.5 %shard_map.77 = (f32[10,16,2048]{2,1,0:T(8,128)}, f32[3,1,512]{2,1,0:T(1,128)S(1)}) custom-call(s32[3]{0:T(128)S(1)} %copy-done.1, f32[2,256,160]{2,1,0:T(8,128)S(1)} %pad_maximum_fusion.refs_1_, s32[256,1]{1,0:T(8,128)S(1)} %copy.18.refs_2_, s32[256,1]{1,0:T(8,128)S(1)} %copy.19.refs_3_, f32[9,16,1024]{2,1,0:T(8,128)S(1)} %collective-permute-done.refs_4_.refs_16_, ...), custom_call_target="tpu_custom_call" | custom-call | flops 49152000 | bytes 5242880 | tf_op jit(solution)/shard_map/pallas_call | solution.py:308
  74.9 0.0 collective-permute-done.5.refs_10_
  74.9 0.0 collective-permute-done.6.refs_12_
  74.9 0.0 collective-permute-done.7.refs_13_
  75.0 0.0 collective-permute-done.9.refs_15_
  75.0 0.0 collective-permute-done.8.refs_14_
  75.0 0.0 copy-start.2
  75.0 0.8 copy-done.2
  75.8 26.6 %shard_map.78 = (f32[10,16,2048]{2,1,0:T(8,128)}, f32[3,1,512]{2,1,0:T(1,128)S(1)}) custom-call(s32[3]{0:T(128)S(1)} %copy-done.1, f32[2,256,160]{2,1,0:T(8,128)S(1)} %pad_maximum_fusion.refs_1_, s32[256,1]{1,0:T(8,128)S(1)} %copy.18.refs_2_, s32[256,1]{1,0:T(8,128)S(1)} %copy.19.refs_3_, ...), custom_call_target="tpu_custom_call", output_to_operand_aliasing={{0}: (22, {})} | custom-call | flops 73728000 | bytes 7864320 | tf_op jit(solution)/shard_map/pallas_call | solution.py:308
  102.5 0.7 collective-permute-start.10
  103.2 3.0 %collective-permute-done.10 = f32[3,256]{1,0:T(4,128)S(1)} collective-permute-done((f32[3,256]{1,0:T(4,128)S(1)}, f32[3,256]{1,0:T(4,128)S(1)}, u32[]{:S(2)}, u32[]{:S(2)}) %collective-permute-start.10) | collective-permute-done | bytes 3104 | tf_op jit(solution)/shard_map/ppermute | solution.py:357
  106.2 0.6 bitcast_add_fusion
  (8 shorter events, 0.1 us)
Async XLA Ops:
  0.6 5.3 %copy-start = (f32[10,16,2048]{2,1,0:T(8,128)S(1)}, f32[10,16,2048]{2,1,0:T(8,128)}, u32[]{:S(2)}) copy-start(f32[10,16,2048]{2,1,0:T(8,128)} %refs_17_.1) | copy-start | bytes 3932164
  3.0 8.6 %copy-start.6 = (s32[256]{0:T(256)S(1)}, s32[256]{0:T(256)}, u32[]{:S(2)}) copy-start(s32[256]{0:T(256)} %param.10) | copy-start | bytes 3076
  3.0 17.7 %collective-permute-start.2 = (f32[10,16,1024]{2,1,0:T(8,128)S(1)}, f32[10,16,1024]{2,1,0:T(8,128)S(1)}, u32[]{:S(2)}, u32[]{:S(2)}) collective-permute-start(f32[10,16,1024]{2,1,0:T(8,128)S(1)} %get-tuple-element.21), channel_id=1, source_target_pairs={{0,1},{1,0},{2,3},{3,2},{4,5},{5,4},{6,7},{7,6},{8,9},{9,8},{10,11... | collective-permute-start | bytes 1966088 | tf_op jit(solution)/shard_map/ppermute | solution.py:245
  7.1 19.2 %copy-start.4 = (s32[256]{0:T(256)S(1)}, s32[256]{0:T(256)}, u32[]{:S(2)}) copy-start(s32[256]{0:T(256)} %param.9) | copy-start | bytes 3076
  7.1 19.2 %copy-start.5 = (s32[256,1]{0,1:T(1,128)S(1)}, s32[256,1]{0,1:T(1,128)}, u32[]{:S(2)}) copy-start(s32[256,1]{0,1:T(1,128)} %param.8) | copy-start | bytes 3076
  7.1 22.6 %collective-permute-start = (f32[9,16,1024]{2,1,0:T(8,128)}, f32[9,16,1024]{2,1,0:T(8,128)S(1)}, u32[]{:S(2)}, u32[]{:S(2)}) collective-permute-start(f32[9,16,1024]{2,1,0:T(8,128)} %get-tuple-element.23), channel_id=1, source_target_pairs={{0,2},{2,4},{4,6},{6,8},{8,10},{10,12},{12,14},{14,16},{16,18},{18... | collective-permute-start | bytes 1769480 | tf_op jit(solution)/shard_map/ppermute | solution.py:240
  7.1 22.7 %collective-permute-start.1 = (f32[9,16,1024]{2,1,0:T(8,128)}, f32[9,16,1024]{2,1,0:T(8,128)S(1)}, u32[]{:S(2)}, u32[]{:S(2)}) collective-permute-start(f32[9,16,1024]{2,1,0:T(8,128)} %get-tuple-element.22), channel_id=1, source_target_pairs={{0,30},{2,0},{4,2},{6,4},{8,6},{10,8},{12,10},{14,12},{16,14},{18,... | collective-permute-start | bytes 1769480 | tf_op jit(solution)/shard_map/ppermute | solution.py:241
  20.7 5.9 %copy-start.3 = (f32[8,256]{1,0:T(8,128)S(1)}, f32[8,256]{1,0:T(8,128)}, u32[]{:S(2)}) copy-start(f32[8,256]{1,0:T(8,128)} %param.11) | copy-start | bytes 24580
  21.8 12.4 %collective-permute-start.3 = (f32[9,16,1024]{2,1,0:T(8,128)}, f32[9,16,1024]{2,1,0:T(8,128)}, u32[]{:S(2)}, u32[]{:S(2)}) collective-permute-start(f32[9,16,1024]{2,1,0:T(8,128)} %get-tuple-element.27), channel_id=1, source_target_pairs={{0,2},{2,4},{4,6},{6,8},{8,10},{10,12},{12,14},{14,16},{16,18},{18... | collective-permute-start | bytes 1769480 | tf_op jit(solution)/shard_map/ppermute | solution.py:240
  21.8 12.5 %collective-permute-start.4 = (f32[9,16,1024]{2,1,0:T(8,128)}, f32[9,16,1024]{2,1,0:T(8,128)}, u32[]{:S(2)}, u32[]{:S(2)}) collective-permute-start(f32[9,16,1024]{2,1,0:T(8,128)} %get-tuple-element.26), channel_id=1, source_target_pairs={{0,30},{2,0},{4,2},{6,4},{8,6},{10,8},{12,10},{14,12},{16,14},{18,... | collective-permute-start | bytes 1769480 | tf_op jit(solution)/shard_map/ppermute | solution.py:241
  26.6 48.3 %collective-permute-start.8 = (f32[10,16,1024]{2,1,0:T(8,128)}, f32[10,16,1024]{2,1,0:T(8,128)S(1)}, u32[]{:S(2)}, u32[]{:S(2)}) collective-permute-start(f32[10,16,1024]{2,1,0:T(8,128)} %get-tuple-element.9), channel_id=1, source_target_pairs={{0,1},{1,0},{2,3},{3,2},{4,5},{5,4},{6,7},{7,6},{8,9},{9,8},{10,11... | collective-permute-start | bytes 1966088 | tf_op jit(solution)/shard_map/ppermute | solution.py:245
  29.8 25.6 %copy-start.1 = (s32[3]{0:T(128)S(1)}, s32[3]{0:T(128)}, u32[]{:S(2)}) copy-start(s32[3]{0:T(128)} %refs_0_.3) | copy-start | bytes 40
  29.8 45.1 %collective-permute-start.5 = (f32[9,16,1024]{2,1,0:T(8,128)S(1)}, f32[9,16,1024]{2,1,0:T(8,128)S(1)}, u32[]{:S(2)}, u32[]{:S(2)}) collective-permute-start(f32[9,16,1024]{2,1,0:T(8,128)S(1)} %get-tuple-element.25), channel_id=1, source_target_pairs={{0,2},{2,4},{4,6},{6,8},{8,10},{10,12},{12,14},{14,16},{16,18},{18... | collective-permute-start | bytes 1769480 | tf_op jit(solution)/shard_map/ppermute | solution.py:240
  29.9 45.1 %collective-permute-start.7 = (f32[9,16,1024]{2,1,0:T(8,128)S(1)}, f32[9,16,1024]{2,1,0:T(8,128)S(1)}, u32[]{:S(2)}, u32[]{:S(2)}) collective-permute-start(f32[9,16,1024]{2,1,0:T(8,128)S(1)} %get-tuple-element.25), channel_id=1, source_target_pairs={{0,3},{1,2},{2,5},{3,4},{4,7},{5,6},{6,9},{7,8},{8,11},{9,10},{10,... | collective-permute-start | bytes 1769480 | tf_op jit(solution)/shard_map/ppermute | solution.py:266
  34.3 40.7 %collective-permute-start.6 = (f32[9,16,1024]{2,1,0:T(8,128)S(1)}, f32[9,16,1024]{2,1,0:T(8,128)S(1)}, u32[]{:S(2)}, u32[]{:S(2)}) collective-permute-start(f32[9,16,1024]{2,1,0:T(8,128)S(1)} %get-tuple-element.24), channel_id=1, source_target_pairs={{0,30},{2,0},{4,2},{6,4},{8,6},{10,8},{12,10},{14,12},{16,14},{18,... | collective-permute-start | bytes 1769480 | tf_op jit(solution)/shard_map/ppermute | solution.py:241
  34.3 40.6 %collective-permute-start.9 = (f32[9,16,1024]{2,1,0:T(8,128)S(1)}, f32[9,16,1024]{2,1,0:T(8,128)S(1)}, u32[]{:S(2)}, u32[]{:S(2)}) collective-permute-start(f32[9,16,1024]{2,1,0:T(8,128)S(1)} %get-tuple-element.24), channel_id=1, source_target_pairs={{0,31},{1,30},{2,1},{3,0},{4,3},{5,2},{6,5},{7,4},{8,7},{9,6},{10,... | collective-permute-start | bytes 1769480 | tf_op jit(solution)/shard_map/ppermute | solution.py:266
  75.0 0.8 copy-start.2
  102.5 3.7 %collective-permute-start.10 = (f32[3,256]{1,0:T(4,128)S(1)}, f32[3,256]{1,0:T(4,128)S(1)}, u32[]{:S(2)}, u32[]{:S(2)}) collective-permute-start(f32[3,256]{1,0:T(4,128)S(1)} %bitcast.24), channel_id=1, source_target_pairs={{0,1},{1,0},{2,3},{3,2},{4,5},{5,4},{6,7},{7,6},{8,9},{9,8},{10,11... | collective-permute-start | bytes 9224 | tf_op jit(solution)/shard_map/ppermute | solution.py:357

commit v5 on v3

--- a/solution.py
+++ b/solution.py
@@ -49,7 +49,8 @@
         weights = select_ref[dx]
         high = weights.astype(jnp.bfloat16)
         rest = (weights - high.astype(jnp.float32)).astype(jnp.bfloat16)
-        chosen[dx] = jnp.concatenate([high, high, rest], axis=1)
+        slots = weights.shape[0]
+        chosen[dx * slots : (dx + 1) * slots] = jnp.concatenate([high, high, rest], axis=1)
     for copy in copies:
         copy.wait()
 
@@ -67,13 +68,13 @@
             at = p + HALO - 1
             for b in range(bands):
                 for r in range(0, rows, 8):
-                    for x in range(0, span, 512):
+                    for x in range(0, span, 256):
                         def plane(k):
-                            return field[at + k, b * rows + r : b * rows + r + 8, x : x + 512]
+                            return field[at + k, b * rows + r : b * rows + r + 8, x : x + 256]
 
                         v = taps(plane(0), plane(d) + plane(-d), plane(d2) + plane(-d2))
                         for place in places[b]:
-                            along[p, place + r : place + r + 8, x : x + 512] = v
+                            along[p, place + r : place + r + 8, x : x + 256] = v
             return c
 
         lax.fori_loop(0, depth + 2, z_body, 0)
@@ -163,7 +164,7 @@
                 trace = flat + hzz
                 squares = 0.0625 * (zy * zy + zx * zx + yx * yx)
                 minors = hxx * hyy + flat * hzz - squares
-                value = (trace * trace * (1.0 / 3.0) - minors) / (1.0 + jnp.exp(trace))
+                value = (trace * trace * (1.0 / 3.0) - minors) * (0.5 - 0.5 * jnp.tanh(0.5 * trace))
                 lanes = slice((j - 1) * LANES, j * LANES)
                 resp[z, r : r + 8, lanes] = jnp.maximum(resp[z, r : r + 8, lanes], value)
                 feature[pl.ds(pl.multiple_of(z * rows + r, 8), 8), lanes] = value
@@ -190,11 +191,14 @@
             where = lax.broadcasted_iota(jnp.int32, (slots, chunk), 1) + x0
             where = where + (first_tile + 1) * LANES
             where = jnp.where(where >= width, where - width, where)
+            picked = jnp.dot(chosen[...], block, preferred_element_type=jnp.float32)
+            kept_cells = 0.0
             for dx in range(2):
                 cell = xcell + dx
                 cell = jnp.where(cell == width, 0, cell)
-                picked = jnp.dot(chosen[dx], block, preferred_element_type=jnp.float32)
-                acc = acc + jnp.sum(jnp.where(where == cell, picked, 0.0), axis=1, keepdims=True)
+                corner = picked[dx * slots : (dx + 1) * slots]
+                kept_cells = kept_cells + jnp.where(where == cell, corner, 0.0)
+            acc = acc + jnp.sum(kept_cells, axis=1, keepdims=True)
             return acc
 
         partial = lax.fori_loop(0, kept // chunk, gather_body, jnp.zeros((slots, 1), jnp.float32))
@@ -230,7 +234,7 @@
     depth, rows, width = density.shape
     groups = lax.axis_size("gy")
 
-    half = width // 2
+    half = width * 5 // 8 // LANES * LANES
 
     def z_sides(block):
         low = lax.ppermute(block[depth - HALO :], "gz", ring("gz", 1))
@@ -281,6 +285,7 @@
     vmem = pl.BlockSpec(memory_space=pltpu.VMEM)
     anywhere = pl.BlockSpec(memory_space=pl.ANY)
     half_tiles = half // LANES
+    rest_tiles = width // LANES - half_tiles
 
     def run(tiles, first_tile, pieces, parts, onto):
         cells = depth * rows * tiles * LANES
@@ -308,7 +313,7 @@
                 pltpu.VMEM((depth + 2, 3 * rows, tiles * LANES), jnp.float32),
                 pltpu.VMEM((depth + 2, rows + 16, tiles * LANES), jnp.float32),
                 pltpu.VMEM((depth * rows, (tiles - 2) * LANES), jnp.float32),
-                pltpu.VMEM((2, base_cell.shape[0], 3 * depth * rows), jnp.bfloat16),
+                pltpu.VMEM((2 * base_cell.shape[0], 3 * depth * rows), jnp.bfloat16),
                 pltpu.VMEM((depth, rows, (tiles - 2) * LANES), jnp.float32),
                 pltpu.SemaphoreType.DMA((len(parts),)),
             ],
@@ -324,12 +329,12 @@
     pieces_a = (((0, 0), half, 0),)
     pieces_b = (
         ((half - edge, half - edge), edge, 0),
-        ((0, half), half, edge),
-        ((0, 0), edge, edge + half),
+        ((0, half), width - half, edge),
+        ((0, 0), edge, edge + width - half),
     )
     response, spread_a = run(half_tiles, 0, pieces_a, parts_a, None)
     response, spread_b = run(
-        half_tiles + 4, half_tiles - 2, pieces_b, parts_a + parts_b + parts_a, response
+        rest_tiles + 4, half_tiles - 2, pieces_b, parts_a + parts_b + parts_a, response
     )
     spread = spread_a + spread_b
 

time: 98.7 us -> 109 us (1.10)
  starting transfers between devices: 25 us -> 34 us
  local copies, waits for them, and re-layouts: 7.79 us -> 9.2 us
    ppermute x4, starting transfers between devices: 5.43 us -> 14.3 us  [z_sides(): low = lax.ppermute(block[depth - HALO:], 'gz', ring('gz', 1))]
    unnamed x13 -> x29, local copies, waits for them, and re-layouts: 0.03 us -> 4.59 us
    slice x4, local copies, waits for them, and re-layouts: 5.12 us -> 2.32 us  [z_sides(): high = lax.ppermute(block[:HALO], 'gz', ring('gz', -1))]
    slice x1, local copies, waits for them, and re-layouts: 2.34 us -> 0.03 us  [per_device(): beside, back = lax.optimization_barrier((beside, density[:, :, half:]))]
    slice x0 -> x1, local copies, waits for them, and re-layouts: none -> 1.3 us  [per_device(): front = density[:, :, :half]]
  transfers between devices with their start and end apart: 11 -> 11, of which waited for: 3 -> 3; matrix products, arithmetic and copies ran while one was open for 6% -> 4% of each run, Pallas kernels for 20% -> 20%
where the time goes in v5:
time: 109 us
  Pallas kernels  45.4 us (42%)
  starting transfers between devices  34 us (31%)
  waiting for transfers between devices  18.1 us (17%)
  local copies, waits for them, and re-layouts  9.2 us (8%)
  other arithmetic  1.14 us (1%)
    pallas_call x2, Pallas kernels, run(): pl.pallas_call(functools.partial(kernel, depth, rows, bands, tiles, first...  45.4 us
    ppermute x2, waiting for transfers between devices, y_sides(): sides = [lax.ppermute(block, 'gy', ring('gy', 1))]  16 us
    ppermute x4, starting transfers between devices, z_sides(): low = lax.ppermute(block[depth - HALO:], 'gz', ring('gz', 1))  14.3 us
    ppermute x4, starting transfers between devices, z_sides(): high = lax.ppermute(block[:HALO], 'gz', ring('gz', -1))  13.3 us
    ppermute x2, starting transfers between devices, y_sides(): sides = [lax.ppermute(block, 'gy', ring('gy', 1))]  4.81 us
    unnamed x29, local copies, waits for them, and re-layouts  4.59 us
    slice x4, local copies, waits for them, and re-layouts, z_sides(): high = lax.ppermute(block[:HALO], 'gz', ring('gz', -1))  2.32 us
  transfers between devices with their start and end apart: 11, of which 3 were waited for; matrix products, arithmetic and copies ran while one was open for 4% of the time, Pallas kernels for 20%

profile of v5, /device:TPU:0, one launch (start us, length us, event | category | flops | bytes accessed | tf_op | source)
XLA Modules:
  0.0 108.7 jit_solution(9744459057600060465)
XLA Ops:
  0.6 0.0 copy-start
  0.6 1.3 %slice.88 = f32[10,16,1280]{2,1,0:T(8,128)S(1)} slice(f32[10,16,2048]{2,1,0:T(8,128)} %refs_17_), slice={[0:10], [0:16], [0:1280]} | slice | bytes 1638400 | tf_op jit(solution)/shard_map/slice | solution.py:250
  2.0 3.0 %collective-permute-start = (f32[10,16,1280]{2,1,0:T(8,128)S(1)}, f32[10,16,1280]{2,1,0:T(8,128)S(1)}, u32[]{:S(2)}, u32[]{:S(2)}) collective-permute-start(f32[10,16,1280]{2,1,0:T(8,128)S(1)} %slice.88), channel_id=1, source_target_pairs={{0,1},{1,0},{2,3},{3,2},{4,5},{5,4},{6,7},{7,6},{8,9},{9,8},{10,11... | collective-permute-start | bytes 2457608 | tf_op jit(solution)/shard_map/ppermute | solution.py:245
  5.0 0.0 copy-done
  5.0 0.1 fusion
  5.1 0.1 collective-permute-start.2
  5.2 4.4 %collective-permute-start.3 = (f32[9,16,1280]{2,1,0:T(8,128)S(1)}, f32[9,16,1280]{2,1,0:T(8,128)S(1)}, u32[]{:S(2)}, u32[]{:S(2)}) collective-permute-start(f32[9,16,1280]{2,1,0:T(8,128)S(1)} %get-tuple-element.34), channel_id=1, source_target_pairs={{0,30},{2,0},{4,2},{6,4},{8,6},{10,8},{12,10},{14,12},{16,14},{18,... | collective-permute-start | bytes 2211848 | tf_op jit(solution)/shard_map/ppermute | solution.py:241
  9.6 0.0 copy-start.13
  9.7 0.0 copy-start.10
  9.7 13.5 %collective-permute-done.refs_8_.refs_20_ = f32[10,16,1280]{2,1,0:T(8,128)S(1)} collective-permute-done((f32[10,16,1280]{2,1,0:T(8,128)S(1)}, f32[10,16,1280]{2,1,0:T(8,128)S(1)}, u32[]{:S(2)}, u32[]{:S(2)}) %collective-permute-start) | collective-permute-done | bytes 819232 | tf_op jit(solution)/shard_map/ppermute | solution.py:245
  23.2 0.1 fusion.1
  23.4 0.1 collective-permute-start.4
  23.4 4.4 %collective-permute-start.5 = (f32[9,16,1280]{2,1,0:T(8,128)S(1)}, f32[9,16,1280]{2,1,0:T(8,128)S(1)}, u32[]{:S(2)}, u32[]{:S(2)}) collective-permute-start(f32[9,16,1280]{2,1,0:T(8,128)S(1)} %get-tuple-element.36), channel_id=1, source_target_pairs={{0,30},{2,0},{4,2},{6,4},{8,6},{10,8},{12,10},{14,12},{16,14},{18,... | collective-permute-start | bytes 2211848 | tf_op jit(solution)/shard_map/ppermute | solution.py:241
  27.8 0.0 copy-done.13
  27.9 1.8 %collective-permute-start.1 = (f32[10,16,768]{2,1,0:T(8,128)S(1)}, f32[10,16,768]{2,1,0:T(8,128)S(1)}, u32[]{:S(2)}, u32[]{:S(2)}) collective-permute-start(f32[10,16,768]{2,1,0:T(8,128)S(1)} %slice.89), channel_id=1, source_target_pairs={{0,1},{1,0},{2,3},{3,2},{4,5},{5,4},{6,7},{7,6},{8,9},{9,8},{10,11... | collective-permute-start | bytes 1474568 | tf_op jit(solution)/shard_map/ppermute | solution.py:245
  29.7 0.0 copy-done.10
  29.7 1.0 fusion.3
  30.7 0.0 collective-permute-done.2.refs_4_.refs_16_
  30.7 0.1 collective-permute-start.6
  30.8 0.0 collective-permute-done.3.refs_6_.refs_18_
  30.8 0.0 copy-start.2
  30.8 0.9 copy-done.2
  31.6 4.4 %collective-permute-start.7 = (f32[9,16,768]{2,1,0:T(8,128)}, f32[9,16,768]{2,1,0:T(8,128)}, u32[]{:S(2)}, u32[]{:S(2)}) collective-permute-start(f32[9,16,768]{2,1,0:T(8,128)} %get-tuple-element.40), channel_id=1, source_target_pairs={{0,30},{2,0},{4,2},{6,4},{8,6},{10,8},{12,10},{14,12},{16,14},{18,... | collective-permute-start | bytes 1327112 | tf_op jit(solution)/shard_map/ppermute | solution.py:241
  36.1 2.4 %collective-permute-done.1.refs_14_ = f32[10,16,768]{2,1,0:T(8,128)S(1)} collective-permute-done((f32[10,16,768]{2,1,0:T(8,128)S(1)}, f32[10,16,768]{2,1,0:T(8,128)S(1)}, u32[]{:S(2)}, u32[]{:S(2)}) %collective-permute-start.1) | collective-permute-done | bytes 491552 | tf_op jit(solution)/shard_map/ppermute | solution.py:245
  38.5 0.0 collective-permute-done.4.refs_7_.refs_19_
  38.5 0.9 copy-done.4
  39.4 0.0 collective-permute-done.5.refs_9_.refs_21_
  39.4 0.9 copy-done.6
  40.3 1.0 fusion.2
  41.3 14.2 %collective-permute-start.8 = (f32[9,16,768]{2,1,0:T(8,128)}, f32[9,16,768]{2,1,0:T(8,128)}, u32[]{:S(2)}, u32[]{:S(2)}) collective-permute-start(f32[9,16,768]{2,1,0:T(8,128)} %get-tuple-element.39), channel_id=1, source_target_pairs={{0,2},{2,4},{4,6},{6,8},{8,10},{10,12},{12,14},{14,16},{16,18},{18... | collective-permute-start | bytes 1327112 | tf_op jit(solution)/shard_map/ppermute | solution.py:240
  55.5 0.0 collective-permute-start.9
  55.5 0.0 copy-done.11
  55.5 0.1 copy.18.refs_2_
  55.7 0.8 copy.19.refs_3_
  56.5 0.5 select_add_fusion.1
  57.0 0.6 copy-done.3
  57.6 0.2 copy-done.5
  57.8 0.0 copy-done.8
  57.8 1.1 %copy-done.7 = f32[9,16,1280]{2,1,0:T(8,128)S(1)} copy-done((f32[9,16,1280]{2,1,0:T(8,128)S(1)}, f32[9,16,1280]{2,1,0:T(8,128)}, u32[]{:S(2)}) %copy-start.7) | copy-done | bytes 737304
  58.9 22.0 %shard_map.77 = (f32[10,16,2048]{2,1,0:T(8,128)}, f32[3,1,512]{2,1,0:T(1,128)S(1)}) custom-call(s32[3]{0:T(128)S(1)} %copy-done.9, f32[2,256,160]{2,1,0:T(8,128)S(1)} %pad_maximum_fusion.refs_1_, s32[256,1]{1,0:T(8,128)S(1)} %copy.18.refs_2_, s32[256,1]{1,0:T(8,128)S(1)} %copy-done.8, f32[9,16,1280]{2,1,0:T(8,128)S(1)} %collective-permute-done.2.refs_4_.refs_16_, ...), custom_call_target="tpu_custom_call" | custom-call | flops 61440000 | bytes 6553600 | tf_op jit(solution)/shard_map/pallas_call | solution.py:300
  81.0 0.0 collective-permute-done.6.refs_10_
  81.0 0.0 collective-permute-done.7.refs_12_
  81.0 0.0 collective-permute-done.8.refs_13_
  81.0 0.0 collective-permute-done.9.refs_15_
  81.0 23.4 %shard_map.78 = (f32[10,16,2048]{2,1,0:T(8,128)}, f32[3,1,512]{2,1,0:T(1,128)S(1)}) custom-call(s32[3]{0:T(128)S(1)} %copy-done.9, f32[2,256,160]{2,1,0:T(8,128)S(1)} %pad_maximum_fusion.refs_1_, s32[256,1]{1,0:T(8,128)S(1)} %copy.18.refs_2_, s32[256,1]{1,0:T(8,128)S(1)} %copy-done.8, ...), custom_call_target="tpu_custom_call", output_to_operand_aliasing={{0}: (22, {})} | custom-call | flops 61440000 | bytes 6553600 | tf_op jit(solution)/shard_map/pallas_call | solution.py:300
  104.4 1.6 %collective-permute-start.10 = (f32[3,256]{1,0:T(4,128)S(1)}, f32[3,256]{1,0:T(4,128)S(1)}, u32[]{:S(2)}, u32[]{:S(2)}) collective-permute-start(f32[3,256]{1,0:T(4,128)S(1)} %bitcast.24), channel_id=1, source_target_pairs={{0,1},{1,0},{2,3},{3,2},{4,5},{5,4},{6,7},{7,6},{8,9},{9,8},{10,11... | collective-permute-start | bytes 9224 | tf_op jit(solution)/shard_map/ppermute | solution.py:349
  106.0 2.1 %collective-permute-done.10 = f32[3,256]{1,0:T(4,128)S(1)} collective-permute-done((f32[3,256]{1,0:T(4,128)S(1)}, f32[3,256]{1,0:T(4,128)S(1)}, u32[]{:S(2)}, u32[]{:S(2)}) %collective-permute-start.10) | collective-permute-done | bytes 3104 | tf_op jit(solution)/shard_map/ppermute | solution.py:349
  108.1 0.6 bitcast_add_fusion
  (22 shorter events, 0.2 us)
Async XLA Ops:
  0.6 4.3 %copy-start = (f32[10,16,2048]{2,1,0:T(8,128)S(1)}, f32[10,16,2048]{2,1,0:T(8,128)}, u32[]{:S(2)}) copy-start(f32[10,16,2048]{2,1,0:T(8,128)} %refs_17_) | copy-start | bytes 3932164
  2.0 21.2 %collective-permute-start = (f32[10,16,1280]{2,1,0:T(8,128)S(1)}, f32[10,16,1280]{2,1,0:T(8,128)S(1)}, u32[]{:S(2)}, u32[]{:S(2)}) collective-permute-start(f32[10,16,1280]{2,1,0:T(8,128)S(1)} %slice.88), channel_id=1, source_target_pairs={{0,1},{1,0},{2,3},{3,2},{4,5},{5,4},{6,7},{7,6},{8,9},{9,8},{10,11... | collective-permute-start | bytes 2457608 | tf_op jit(solution)/shard_map/ppermute | solution.py:245
  5.1 25.6 %collective-permute-start.2 = (f32[9,16,1280]{2,1,0:T(8,128)S(1)}, f32[9,16,1280]{2,1,0:T(8,128)S(1)}, u32[]{:S(2)}, u32[]{:S(2)}) collective-permute-start(f32[9,16,1280]{2,1,0:T(8,128)S(1)} %get-tuple-element.35), channel_id=1, source_target_pairs={{0,2},{2,4},{4,6},{6,8},{8,10},{10,12},{12,14},{14,16},{16,18},{18... | collective-permute-start | bytes 2211848 | tf_op jit(solution)/shard_map/ppermute | solution.py:240
  5.2 25.6 %collective-permute-start.3 = (f32[9,16,1280]{2,1,0:T(8,128)S(1)}, f32[9,16,1280]{2,1,0:T(8,128)S(1)}, u32[]{:S(2)}, u32[]{:S(2)}) collective-permute-start(f32[9,16,1280]{2,1,0:T(8,128)S(1)} %get-tuple-element.34), channel_id=1, source_target_pairs={{0,30},{2,0},{4,2},{6,4},{8,6},{10,8},{12,10},{14,12},{16,14},{18,... | collective-permute-start | bytes 2211848 | tf_op jit(solution)/shard_map/ppermute | solution.py:241
  9.6 18.2 %copy-start.13 = (s32[256]{0:T(256)S(1)}, s32[256]{0:T(256)}, u32[]{:S(2)}) copy-start(s32[256]{0:T(256)} %param.10) | copy-start | bytes 3076
  9.7 20.0 %copy-start.10 = (f32[8,256]{1,0:T(8,128)S(1)}, f32[8,256]{1,0:T(8,128)}, u32[]{:S(2)}) copy-start(f32[8,256]{1,0:T(8,128)} %param.11) | copy-start | bytes 24580
  23.2 33.8 %copy-start.1 = (f32[10,16,1280]{2,1,0:T(8,128)}, f32[10,16,1280]{2,1,0:T(8,128)S(1)}, u32[]{:S(2)}) copy-start(f32[10,16,1280]{2,1,0:T(8,128)S(1)} %collective-permute-done.refs_8_.refs_20_) | copy-start | bytes 2457604
  23.4 15.2 %collective-permute-start.4 = (f32[9,16,1280]{2,1,0:T(8,128)S(1)}, f32[9,16,1280]{2,1,0:T(8,128)S(1)}, u32[]{:S(2)}, u32[]{:S(2)}) collective-permute-start(f32[9,16,1280]{2,1,0:T(8,128)S(1)} %get-tuple-element.37), channel_id=1, source_target_pairs={{0,2},{2,4},{4,6},{6,8},{8,10},{10,12},{12,14},{14,16},{16,18},{18... | collective-permute-start | bytes 2211848 | tf_op jit(solution)/shard_map/ppermute | solution.py:240
  23.4 16.0 %collective-permute-start.5 = (f32[9,16,1280]{2,1,0:T(8,128)S(1)}, f32[9,16,1280]{2,1,0:T(8,128)S(1)}, u32[]{:S(2)}, u32[]{:S(2)}) collective-permute-start(f32[9,16,1280]{2,1,0:T(8,128)S(1)} %get-tuple-element.36), channel_id=1, source_target_pairs={{0,30},{2,0},{4,2},{6,4},{8,6},{10,8},{12,10},{14,12},{16,14},{18,... | collective-permute-start | bytes 2211848 | tf_op jit(solution)/shard_map/ppermute | solution.py:241
  27.9 10.6 %collective-permute-start.1 = (f32[10,16,768]{2,1,0:T(8,128)S(1)}, f32[10,16,768]{2,1,0:T(8,128)S(1)}, u32[]{:S(2)}, u32[]{:S(2)}) collective-permute-start(f32[10,16,768]{2,1,0:T(8,128)S(1)} %slice.89), channel_id=1, source_target_pairs={{0,1},{1,0},{2,3},{3,2},{4,5},{5,4},{6,7},{7,6},{8,9},{9,8},{10,11... | collective-permute-start | bytes 1474568 | tf_op jit(solution)/shard_map/ppermute | solution.py:245
  30.7 24.8 %copy-start.11 = (s32[256]{0:T(256)S(1)}, s32[256]{0:T(256)}, u32[]{:S(2)}) copy-start(s32[256]{0:T(256)} %param.9) | copy-start | bytes 3076
  30.7 24.8 %copy-start.12 = (s32[256,1]{0,1:T(1,128)S(1)}, s32[256,1]{0,1:T(1,128)}, u32[]{:S(2)}) copy-start(s32[256,1]{0,1:T(1,128)} %param.8) | copy-start | bytes 3076
  30.7 50.2 %collective-permute-start.6 = (f32[9,16,768]{2,1,0:T(8,128)}, f32[9,16,768]{2,1,0:T(8,128)}, u32[]{:S(2)}, u32[]{:S(2)}) collective-permute-start(f32[9,16,768]{2,1,0:T(8,128)} %get-tuple-element.41), channel_id=1, source_target_pairs={{0,2},{2,4},{4,6},{6,8},{8,10},{10,12},{12,14},{14,16},{16,18},{18... | collective-permute-start | bytes 1327112 | tf_op jit(solution)/shard_map/ppermute | solution.py:240
  30.8 0.9 copy-start.2
  31.6 49.3 %collective-permute-start.7 = (f32[9,16,768]{2,1,0:T(8,128)}, f32[9,16,768]{2,1,0:T(8,128)}, u32[]{:S(2)}, u32[]{:S(2)}) collective-permute-start(f32[9,16,768]{2,1,0:T(8,128)} %get-tuple-element.40), channel_id=1, source_target_pairs={{0,30},{2,0},{4,2},{6,4},{8,6},{10,8},{12,10},{14,12},{16,14},{18,... | collective-permute-start | bytes 1327112 | tf_op jit(solution)/shard_map/ppermute | solution.py:241
  38.5 0.9 copy-start.4
  39.4 0.9 copy-start.6
  41.3 15.7 %copy-start.9 = (s32[3]{0:T(128)S(1)}, s32[3]{0:T(128)}, u32[]{:S(2)}) copy-start(s32[3]{0:T(128)} %refs_0_.3) | copy-start | bytes 40
  41.3 39.6 %collective-permute-start.8 = (f32[9,16,768]{2,1,0:T(8,128)}, f32[9,16,768]{2,1,0:T(8,128)}, u32[]{:S(2)}, u32[]{:S(2)}) collective-permute-start(f32[9,16,768]{2,1,0:T(8,128)} %get-tuple-element.39), channel_id=1, source_target_pairs={{0,2},{2,4},{4,6},{6,8},{8,10},{10,12},{12,14},{14,16},{16,18},{18... | collective-permute-start | bytes 1327112 | tf_op jit(solution)/shard_map/ppermute | solution.py:240
  55.5 25.5 %collective-permute-start.9 = (f32[9,16,768]{2,1,0:T(8,128)}, f32[9,16,768]{2,1,0:T(8,128)}, u32[]{:S(2)}, u32[]{:S(2)}) collective-permute-start(f32[9,16,768]{2,1,0:T(8,128)} %get-tuple-element.38), channel_id=1, source_target_pairs={{0,30},{2,0},{4,2},{6,4},{8,6},{10,8},{12,10},{14,12},{16,14},{18,... | collective-permute-start | bytes 1327112 | tf_op jit(solution)/shard_map/ppermute | solution.py:241
  56.5 1.1 %copy-start.3 = (f32[9,16,1280]{2,1,0:T(8,128)S(1)}, f32[9,16,1280]{2,1,0:T(8,128)}, u32[]{:S(2)}) copy-start(f32[9,16,1280]{2,1,0:T(8,128)} %copy-done.2) | copy-start | bytes 2211844
  56.5 1.3 %copy-start.5 = (f32[9,16,1280]{2,1,0:T(8,128)S(1)}, f32[9,16,1280]{2,1,0:T(8,128)}, u32[]{:S(2)}) copy-start(f32[9,16,1280]{2,1,0:T(8,128)} %copy-done.4) | copy-start | bytes 2211844
  56.5 1.3 %copy-start.8 = (s32[256,1]{1,0:T(8,128)S(1)}, s32[256,1]{1,0:T(8,128)}, u32[]{:S(2)}) copy-start(s32[256,1]{1,0:T(8,128)} %copy.19.refs_3_) | copy-start | bytes 3076
  57.8 1.1 %copy-start.7 = (f32[9,16,1280]{2,1,0:T(8,128)S(1)}, f32[9,16,1280]{2,1,0:T(8,128)}, u32[]{:S(2)}) copy-start(f32[9,16,1280]{2,1,0:T(8,128)} %copy-done.6) | copy-start | bytes 2211844
  104.4 3.7 %collective-permute-start.10 = (f32[3,256]{1,0:T(4,128)S(1)}, f32[3,256]{1,0:T(4,128)S(1)}, u32[]{:S(2)}, u32[]{:S(2)}) collective-permute-start(f32[3,256]{1,0:T(4,128)S(1)} %bitcast.24), channel_id=1, source_target_pairs={{0,1},{1,0},{2,3},{3,2},{4,5},{5,4},{6,7},{7,6},{8,9},{9,8},{10,11... | collective-permute-start | bytes 9224 | tf_op jit(solution)/shard_map/ppermute | solution.py:349

commit v6 on v5

--- a/solution.py
+++ b/solution.py
@@ -35,9 +35,10 @@
             for i in range(3):
                 src = parts[(n * bands + b) * 3 + i]
                 planes = depth if i == 1 else HALO
+                row = b * rows if src.shape[1] != rows else 0
                 copies.append(
                     pltpu.make_async_copy(
-                        src.at[:, :, pl.ds(low[src.shape[2] == width], size)],
+                        src.at[:, pl.ds(row, rows), pl.ds(low[src.shape[2] == width], size)],
                         field.at[pl.ds(starts[i], planes), pl.ds(b * rows, rows), pl.ds(to, size)],
                         sems.at[len(copies)],
                     )
@@ -256,11 +257,10 @@
     for band in beside:
         low, high = z_sides(band)
         parts_a += [low, band, high]
-    low, high = z_sides(back)
+    beside_b, parts_a = lax.optimization_barrier((beside_b, parts_a))
+    low, high = z_sides(jnp.concatenate([back] + beside_b, axis=1))
     parts_b = [low, density, high]
-    beside_b, parts_a = lax.optimization_barrier((beside_b, parts_a))
     for band in beside_b:
-        low, high = z_sides(band)
         parts_b += [low, band, high]
     bands = 1 + len(beside)
 

time: 109 us -> 99.6 us (0.914)
  starting transfers between devices: 34 us -> 20.1 us
  waiting for transfers between devices: 18.1 us -> 23.5 us
    ppermute x4 -> x3, starting transfers between devices: 14.3 us -> 4.89 us  [z_sides(): low = lax.ppermute(block[depth - HALO:], 'gz', ring('gz', 1))]
    ppermute x2, waiting for transfers between devices: 16 us -> 21.4 us  [y_sides(): sides = [lax.ppermute(block, 'gy', ring('gy', 1))]]
    ppermute x4 -> x3, starting transfers between devices: 13.3 us -> 8.86 us  [z_sides(): high = lax.ppermute(block[:HALO], 'gz', ring('gz', -1))]
    slice x4 -> x3, local copies, waits for them, and re-layouts: 2.32 us -> 1.72 us  [z_sides(): high = lax.ppermute(block[:HALO], 'gz', ring('gz', -1))]
    unnamed x29 -> x28, local copies, waits for them, and re-layouts: 4.59 us -> 4.58 us
  transfers between devices with their start and end apart: 11 -> 9, of which waited for: 3 -> 3; matrix products, arithmetic and copies ran while one was open for 4% -> 2% of each run, Pallas kernels for 20% -> 22%
where the time goes in v6:
time: 99.6 us; the launch traced here: 99.5 us
  Pallas kernels  45.2 us (45%)
  waiting for transfers between devices  23.5 us (24%)
  starting transfers between devices  20.1 us (20%)
  local copies, waits for them, and re-layouts  8.65 us (9%)
  other arithmetic  1.15 us (1%)
    pallas_call x2, Pallas kernels, run(): pl.pallas_call(functools.partial(kernel, depth, rows, bands, tiles, first...  45.2 us
    ppermute x2, waiting for transfers between devices, y_sides(): sides = [lax.ppermute(block, 'gy', ring('gy', 1))]  21.4 us
    ppermute x3, starting transfers between devices, z_sides(): high = lax.ppermute(block[:HALO], 'gz', ring('gz', -1))  8.86 us
    ppermute x3, starting transfers between devices, z_sides(): low = lax.ppermute(block[depth - HALO:], 'gz', ring('gz', 1))  4.89 us
    ppermute x2, starting transfers between devices, y_sides(): sides = [lax.ppermute(block, 'gy', ring('gy', 1))]  4.74 us
    unnamed x28, local copies, waits for them, and re-layouts  4.58 us
    ppermute x1, waiting for transfers between devices, per_device(): lax.ppermute(share((me + step) % groups), 'gy', ring('gy', step))  2.12 us
  transfers between devices with their start and end apart: 9, of which 3 were waited for; matrix products, arithmetic and copies ran while one was open for 2% of the time, Pallas kernels for 22%

profile of v6, /device:TPU:0, one launch (start us, length us, event | category | flops | bytes accessed | tf_op | source)
XLA Modules:
  0.0 99.5 jit_solution(3002927091078220046)
XLA Ops:
  0.6 0.0 copy-start
  0.6 1.3 %slice.82 = f32[10,16,1280]{2,1,0:T(8,128)S(1)} slice(f32[10,16,2048]{2,1,0:T(8,128)} %refs_17_), slice={[0:10], [0:16], [0:1280]} | slice | bytes 1638400 | tf_op jit(solution)/shard_map/slice | solution.py:251
  2.0 3.0 %collective-permute-start = (f32[10,16,1280]{2,1,0:T(8,128)S(1)}, f32[10,16,1280]{2,1,0:T(8,128)S(1)}, u32[]{:S(2)}, u32[]{:S(2)}) collective-permute-start(f32[10,16,1280]{2,1,0:T(8,128)S(1)} %slice.82), channel_id=1, source_target_pairs={{0,1},{1,0},{2,3},{3,2},{4,5},{5,4},{6,7},{7,6},{8,9},{9,8},{10,11... | collective-permute-start | bytes 2457608 | tf_op jit(solution)/shard_map/ppermute | solution.py:246
  5.0 0.0 copy-done
  5.0 0.2 fusion
  5.1 0.1 collective-permute-start.2
  5.2 4.4 %collective-permute-start.3 = (f32[9,16,1280]{2,1,0:T(8,128)S(1)}, f32[9,16,1280]{2,1,0:T(8,128)S(1)}, u32[]{:S(2)}, u32[]{:S(2)}) collective-permute-start(f32[9,16,1280]{2,1,0:T(8,128)S(1)} %get-tuple-element.34), channel_id=1, source_target_pairs={{0,30},{2,0},{4,2},{6,4},{8,6},{10,8},{12,10},{14,12},{16,14},{18,... | collective-permute-start | bytes 2211848 | tf_op jit(solution)/shard_map/ppermute | solution.py:242
  9.7 0.0 copy-start.12
  9.7 13.5 %collective-permute-done.refs_8_.refs_20_ = f32[10,16,1280]{2,1,0:T(8,128)S(1)} collective-permute-done((f32[10,16,1280]{2,1,0:T(8,128)S(1)}, f32[10,16,1280]{2,1,0:T(8,128)S(1)}, u32[]{:S(2)}, u32[]{:S(2)}) %collective-permute-start) | collective-permute-done | bytes 819232 | tf_op jit(solution)/shard_map/ppermute | solution.py:246
  23.2 0.1 fusion.2
  23.4 0.1 collective-permute-start.4
  23.4 4.4 %collective-permute-start.5 = (f32[9,16,1280]{2,1,0:T(8,128)S(1)}, f32[9,16,1280]{2,1,0:T(8,128)S(1)}, u32[]{:S(2)}, u32[]{:S(2)}) collective-permute-start(f32[9,16,1280]{2,1,0:T(8,128)S(1)} %get-tuple-element.38), channel_id=1, source_target_pairs={{0,30},{2,0},{4,2},{6,4},{8,6},{10,8},{12,10},{14,12},{16,14},{18,... | collective-permute-start | bytes 2211848 | tf_op jit(solution)/shard_map/ppermute | solution.py:242
  27.9 1.7 %collective-permute-start.1 = (f32[10,16,768]{2,1,0:T(8,128)S(1)}, f32[10,16,768]{2,1,0:T(8,128)S(1)}, u32[]{:S(2)}, u32[]{:S(2)}) collective-permute-start(f32[10,16,768]{2,1,0:T(8,128)S(1)} %slice.83), channel_id=1, source_target_pairs={{0,1},{1,0},{2,3},{3,2},{4,5},{5,4},{6,7},{7,6},{8,9},{9,8},{10,11... | collective-permute-start | bytes 1474568 | tf_op jit(solution)/shard_map/ppermute | solution.py:246
  29.6 0.0 copy-done.12
  29.7 0.0 collective-permute-done.2.refs_4_.refs_16_
  29.7 0.0 collective-permute-done.3.refs_6_.refs_18_
  29.7 0.0 copy-start.1
  29.7 0.9 copy-done.1
  30.5 7.9 %collective-permute-done.1.refs_14_ = f32[10,16,768]{2,1,0:T(8,128)S(1)} collective-permute-done((f32[10,16,768]{2,1,0:T(8,128)S(1)}, f32[10,16,768]{2,1,0:T(8,128)S(1)}, u32[]{:S(2)}, u32[]{:S(2)}) %collective-permute-start.1) | collective-permute-done | bytes 491552 | tf_op jit(solution)/shard_map/ppermute | solution.py:246
  38.4 0.0 collective-permute-done.4.refs_7_.refs_19_
  38.4 0.0 copy-start.3
  38.4 0.9 copy-done.3
  39.3 0.0 collective-permute-done.5.refs_9_.refs_21_
  39.3 0.9 copy-done.5
  40.2 0.0 copy-start.10
  40.2 0.0 copy-start.11
  40.3 0.0 copy-start.9
  40.3 1.4 %fusion.1 = (f32[9,32,768]{2,1,0:T(8,128)}, f32[9,32,768]{2,1,0:T(8,128)}) fusion(f32[10,32,768]{2,1,0:T(8,128)S(1)} %constant_dynamic-update-slice_fusion), kind=kLoop, calls=%fused_computation.29 | loop fusion | bytes 3538944 | tf_op jit(solution)/shard_map/slice | solution.py:242
  41.7 4.8 %collective-permute-start.6 = (f32[9,32,768]{2,1,0:T(8,128)}, f32[9,32,768]{2,1,0:T(8,128)}, u32[]{:S(2)}, u32[]{:S(2)}) collective-permute-start(f32[9,32,768]{2,1,0:T(8,128)} %get-tuple-element.37), channel_id=1, source_target_pairs={{0,2},{2,4},{4,6},{6,8},{8,10},{10,12},{12,14},{14,16},{16,18},{18... | collective-permute-start | bytes 2654216 | tf_op jit(solution)/shard_map/ppermute | solution.py:241
  46.5 0.0 collective-permute-start.7
  46.5 0.0 copy-done.10
  46.5 0.0 copy-done.11
  46.5 0.1 copy.18.refs_2_
  46.6 0.8 copy.19.refs_3_
  47.5 0.0 copy-done.9
  47.5 0.5 select_add_fusion.1
  48.0 0.0 copy-done.8
  48.0 0.5 copy-done.2
  48.6 0.2 copy-done.4
  48.8 0.0 copy-done.7
  48.8 1.1 %copy-done.6 = f32[9,16,1280]{2,1,0:T(8,128)S(1)} copy-done((f32[9,16,1280]{2,1,0:T(8,128)S(1)}, f32[9,16,1280]{2,1,0:T(8,128)}, u32[]{:S(2)}) %copy-start.6) | copy-done | bytes 737304
  49.9 22.0 %shard_map.77 = (f32[10,16,2048]{2,1,0:T(8,128)}, f32[3,1,512]{2,1,0:T(1,128)S(1)}) custom-call(s32[3]{0:T(128)S(1)} %copy-done.8, f32[2,256,160]{2,1,0:T(8,128)S(1)} %pad_maximum_fusion.refs_1_, s32[256,1]{1,0:T(8,128)S(1)} %copy.18.refs_2_, s32[256,1]{1,0:T(8,128)S(1)} %copy-done.7, f32[9,16,1280]{2,1,0:T(8,128)S(1)} %collective-permute-done.2.refs_4_.refs_16_, ...), custom_call_target="tpu_custom_call" | custom-call | flops 61440000 | bytes 6553600 | tf_op jit(solution)/shard_map/pallas_call | solution.py:300
  71.9 0.0 collective-permute-done.6.refs_10_.refs_13_
  72.0 0.0 collective-permute-done.7.refs_12_.refs_15_
  72.0 23.2 %shard_map.78 = (f32[10,16,2048]{2,1,0:T(8,128)}, f32[3,1,512]{2,1,0:T(1,128)S(1)}) custom-call(s32[3]{0:T(128)S(1)} %copy-done.8, f32[2,256,160]{2,1,0:T(8,128)S(1)} %pad_maximum_fusion.refs_1_, s32[256,1]{1,0:T(8,128)S(1)} %copy.18.refs_2_, s32[256,1]{1,0:T(8,128)S(1)} %copy-done.7, ...), custom_call_target="tpu_custom_call", output_to_operand_aliasing={{0}: (22, {})} | custom-call | flops 61440000 | bytes 6553600 | tf_op jit(solution)/shard_map/pallas_call | solution.py:300
  95.2 1.6 %collective-permute-start.8 = (f32[3,256]{1,0:T(4,128)S(1)}, f32[3,256]{1,0:T(4,128)S(1)}, u32[]{:S(2)}, u32[]{:S(2)}) collective-permute-start(f32[3,256]{1,0:T(4,128)S(1)} %bitcast.24), channel_id=1, source_target_pairs={{0,1},{1,0},{2,3},{3,2},{4,5},{5,4},{6,7},{7,6},{8,9},{9,8},{10,11... | collective-permute-start | bytes 9224 | tf_op jit(solution)/shard_map/ppermute | solution.py:349
  96.8 2.1 %collective-permute-done.8 = f32[3,256]{1,0:T(4,128)S(1)} collective-permute-done((f32[3,256]{1,0:T(4,128)S(1)}, f32[3,256]{1,0:T(4,128)S(1)}, u32[]{:S(2)}, u32[]{:S(2)}) %collective-permute-start.8) | collective-permute-done | bytes 3104 | tf_op jit(solution)/shard_map/ppermute | solution.py:349
  98.9 0.6 bitcast_add_fusion
  (17 shorter events, 0.2 us)
Async XLA Ops:
  0.6 4.3 %copy-start = (f32[10,16,2048]{2,1,0:T(8,128)S(1)}, f32[10,16,2048]{2,1,0:T(8,128)}, u32[]{:S(2)}) copy-start(f32[10,16,2048]{2,1,0:T(8,128)} %refs_17_) | copy-start | bytes 3932164
  2.0 21.2 %collective-permute-start = (f32[10,16,1280]{2,1,0:T(8,128)S(1)}, f32[10,16,1280]{2,1,0:T(8,128)S(1)}, u32[]{:S(2)}, u32[]{:S(2)}) collective-permute-start(f32[10,16,1280]{2,1,0:T(8,128)S(1)} %slice.82), channel_id=1, source_target_pairs={{0,1},{1,0},{2,3},{3,2},{4,5},{5,4},{6,7},{7,6},{8,9},{9,8},{10,11... | collective-permute-start | bytes 2457608 | tf_op jit(solution)/shard_map/ppermute | solution.py:246
  5.1 24.5 %collective-permute-start.2 = (f32[9,16,1280]{2,1,0:T(8,128)S(1)}, f32[9,16,1280]{2,1,0:T(8,128)S(1)}, u32[]{:S(2)}, u32[]{:S(2)}) collective-permute-start(f32[9,16,1280]{2,1,0:T(8,128)S(1)} %get-tuple-element.35), channel_id=1, source_target_pairs={{0,2},{2,4},{4,6},{6,8},{8,10},{10,12},{12,14},{14,16},{16,18},{18... | collective-permute-start | bytes 2211848 | tf_op jit(solution)/shard_map/ppermute | solution.py:241
  5.2 24.5 %collective-permute-start.3 = (f32[9,16,1280]{2,1,0:T(8,128)S(1)}, f32[9,16,1280]{2,1,0:T(8,128)S(1)}, u32[]{:S(2)}, u32[]{:S(2)}) collective-permute-start(f32[9,16,1280]{2,1,0:T(8,128)S(1)} %get-tuple-element.34), channel_id=1, source_target_pairs={{0,30},{2,0},{4,2},{6,4},{8,6},{10,8},{12,10},{14,12},{16,14},{18,... | collective-permute-start | bytes 2211848 | tf_op jit(solution)/shard_map/ppermute | solution.py:242
  9.7 19.9 %copy-start.12 = (s32[256]{0:T(256)S(1)}, s32[256]{0:T(256)}, u32[]{:S(2)}) copy-start(s32[256]{0:T(256)} %param.10) | copy-start | bytes 3076
  23.4 15.1 %collective-permute-start.4 = (f32[9,16,1280]{2,1,0:T(8,128)S(1)}, f32[9,16,1280]{2,1,0:T(8,128)S(1)}, u32[]{:S(2)}, u32[]{:S(2)}) collective-permute-start(f32[9,16,1280]{2,1,0:T(8,128)S(1)} %get-tuple-element.39), channel_id=1, source_target_pairs={{0,2},{2,4},{4,6},{6,8},{8,10},{10,12},{12,14},{14,16},{16,18},{18... | collective-permute-start | bytes 2211848 | tf_op jit(solution)/shard_map/ppermute | solution.py:241
  23.4 15.9 %collective-permute-start.5 = (f32[9,16,1280]{2,1,0:T(8,128)S(1)}, f32[9,16,1280]{2,1,0:T(8,128)S(1)}, u32[]{:S(2)}, u32[]{:S(2)}) collective-permute-start(f32[9,16,1280]{2,1,0:T(8,128)S(1)} %get-tuple-element.38), channel_id=1, source_target_pairs={{0,30},{2,0},{4,2},{6,4},{8,6},{10,8},{12,10},{14,12},{16,14},{18,... | collective-permute-start | bytes 2211848 | tf_op jit(solution)/shard_map/ppermute | solution.py:242
  27.9 10.6 %collective-permute-start.1 = (f32[10,16,768]{2,1,0:T(8,128)S(1)}, f32[10,16,768]{2,1,0:T(8,128)S(1)}, u32[]{:S(2)}, u32[]{:S(2)}) collective-permute-start(f32[10,16,768]{2,1,0:T(8,128)S(1)} %slice.83), channel_id=1, source_target_pairs={{0,1},{1,0},{2,3},{3,2},{4,5},{5,4},{6,7},{7,6},{8,9},{9,8},{10,11... | collective-permute-start | bytes 1474568 | tf_op jit(solution)/shard_map/ppermute | solution.py:246
  29.7 0.9 copy-start.1
  38.4 0.9 copy-start.3
  39.3 0.9 copy-start.5
  40.2 6.2 %copy-start.10 = (s32[256]{0:T(256)S(1)}, s32[256]{0:T(256)}, u32[]{:S(2)}) copy-start(s32[256]{0:T(256)} %param.9) | copy-start | bytes 3076
  40.2 6.2 %copy-start.11 = (s32[256,1]{0,1:T(1,128)S(1)}, s32[256,1]{0,1:T(1,128)}, u32[]{:S(2)}) copy-start(s32[256,1]{0,1:T(1,128)} %param.8) | copy-start | bytes 3076
  40.3 7.2 %copy-start.9 = (f32[8,256]{1,0:T(8,128)S(1)}, f32[8,256]{1,0:T(8,128)}, u32[]{:S(2)}) copy-start(f32[8,256]{1,0:T(8,128)} %param.11) | copy-start | bytes 24580
  41.7 6.4 %copy-start.8 = (s32[3]{0:T(128)S(1)}, s32[3]{0:T(128)}, u32[]{:S(2)}) copy-start(s32[3]{0:T(128)} %refs_0_.3) | copy-start | bytes 40
  41.7 30.3 %collective-permute-start.6 = (f32[9,32,768]{2,1,0:T(8,128)}, f32[9,32,768]{2,1,0:T(8,128)}, u32[]{:S(2)}, u32[]{:S(2)}) collective-permute-start(f32[9,32,768]{2,1,0:T(8,128)} %get-tuple-element.37), channel_id=1, source_target_pairs={{0,2},{2,4},{4,6},{6,8},{8,10},{10,12},{12,14},{14,16},{16,18},{18... | collective-permute-start | bytes 2654216 | tf_op jit(solution)/shard_map/ppermute | solution.py:241
  46.5 25.5 %collective-permute-start.7 = (f32[9,32,768]{2,1,0:T(8,128)}, f32[9,32,768]{2,1,0:T(8,128)}, u32[]{:S(2)}, u32[]{:S(2)}) collective-permute-start(f32[9,32,768]{2,1,0:T(8,128)} %get-tuple-element.36), channel_id=1, source_target_pairs={{0,30},{2,0},{4,2},{6,4},{8,6},{10,8},{12,10},{14,12},{16,14},{18,... | collective-permute-start | bytes 2654216 | tf_op jit(solution)/shard_map/ppermute | solution.py:242
  47.5 1.1 %copy-start.2 = (f32[9,16,1280]{2,1,0:T(8,128)S(1)}, f32[9,16,1280]{2,1,0:T(8,128)}, u32[]{:S(2)}) copy-start(f32[9,16,1280]{2,1,0:T(8,128)} %copy-done.1) | copy-start | bytes 2211844
  47.5 1.3 %copy-start.4 = (f32[9,16,1280]{2,1,0:T(8,128)S(1)}, f32[9,16,1280]{2,1,0:T(8,128)}, u32[]{:S(2)}) copy-start(f32[9,16,1280]{2,1,0:T(8,128)} %copy-done.3) | copy-start | bytes 2211844
  47.5 1.3 %copy-start.7 = (s32[256,1]{1,0:T(8,128)S(1)}, s32[256,1]{1,0:T(8,128)}, u32[]{:S(2)}) copy-start(s32[256,1]{1,0:T(8,128)} %copy.19.refs_3_) | copy-start | bytes 3076
  48.8 1.1 %copy-start.6 = (f32[9,16,1280]{2,1,0:T(8,128)S(1)}, f32[9,16,1280]{2,1,0:T(8,128)}, u32[]{:S(2)}) copy-start(f32[9,16,1280]{2,1,0:T(8,128)} %copy-done.5) | copy-start | bytes 2211844
  95.2 3.7 %collective-permute-start.8 = (f32[3,256]{1,0:T(4,128)S(1)}, f32[3,256]{1,0:T(4,128)S(1)}, u32[]{:S(2)}, u32[]{:S(2)}) collective-permute-start(f32[3,256]{1,0:T(4,128)S(1)} %bitcast.24), channel_id=1, source_target_pairs={{0,1},{1,0},{2,3},{3,2},{4,5},{5,4},{6,7},{7,6},{8,9},{9,8},{10,11... | collective-permute-start | bytes 9224 | tf_op jit(solution)/shard_map/ppermute | solution.py:349
